TPU v7x, 128 devices: a whole 4x4x4 slice. The times are simulated.
128 devices in a mesh: dp: 2 (over y_lo), space: 16 (over x, y_hi, core), chan: 4 (over z).
Axes of the slice: x: 4, y: 4 (y_hi: 2, y_lo: 2; y = y_hi * 2 + y_lo), z: 4, core: 2. Of those that a mesh axis runs over, the one named last changes fastest.
Arguments:
- samples: bfloat16 [2, 64, 64, 32, 256], P('dp', None, 'space', 'chan'), may hold values from -6 to 6
- early_filters: bfloat16 [27, 128, 64], replicated, may hold values from -0.15625 to 0.15625
- deep_filters: bfloat16 [27, 256, 128], P(None, 'chan'), may hold values from -0.109375 to 0.109375
- deep_cotangent: bfloat16 [2, 256, 32, 16, 128], P('dp', 'chan', 'space'), may hold values from -0.09375 to 0.09375
Outputs:
- deep_act: bfloat16 [2, 256, 32, 16, 128], P('dp', 'chan', 'space')
- deep_grad: float32 [27, 256, 128], P(None, 'chan')
- early_grad: float32 [27, 128, 64], replicated
All inputs are finite; a program needn't handle non-finite values.
Results may differ from a plain program's by a relative error of at most 0.0053.
Values may be sent and summed in bfloat16 or wider, within the bound.
A program may use at most 256 MiB of HBM per device.

v0:
```python
import jax
import jax.numpy as jnp
from jax import lax
from jax.sharding import PartitionSpec as P


def with_halo(value, sides, width):
    for axis, dim in sides:
        count, length = (lax.axis_size(axis), value.shape[dim])
        up = [(i, (i + 1) % count) for i in range(count - 1)]
        down = [(j, i) for i, j in up]
        last = lax.slice_in_dim(value, length - width, length, axis=dim)
        first = lax.slice_in_dim(value, 0, width, axis=dim)
        before = lax.ppermute(last, axis, up)
        after = lax.ppermute(first, axis, down)
        value = jnp.concatenate([before, value, after], axis=dim)
    return value


def slope(values):
    gate = jax.nn.sigmoid(values)
    return gate * (1.0 + values * (1.0 - gate))


def tap_offsets(tap_index):
    return (tap_index // 9, tap_index // 3 % 3, tap_index % 3)


def tap_slice(padded, starts, extent):
    return padded[
        :,
        :,
        starts[0] : starts[0] + extent[0],
        starts[1] : starts[1] + extent[1],
        starts[2] : starts[2] + extent[2],
    ]


def forward_conv(padded, filters, extent):
    summed = None
    for tap_index in range(27):
        contrib = jnp.einsum(
            "oc,scxyz->soxyz",
            filters[tap_index],
            tap_slice(padded, tap_offsets(tap_index), extent),
            preferred_element_type=jnp.float32,
        )
        summed = contrib if summed is None else summed + contrib
    return summed


def backward_conv(padded, filters, extent):
    summed = None
    for tap_index in range(27):
        starts = tuple((2 - offset for offset in tap_offsets(tap_index)))
        contrib = jnp.einsum(
            "oc,soxyz->scxyz",
            filters[tap_index],
            tap_slice(padded, starts, extent),
            preferred_element_type=jnp.float32,
        )
        summed = contrib if summed is None else summed + contrib
    return summed


def filter_grad(cotangent, padded, extent):
    return jnp.stack(
        [
            jnp.einsum(
                "soxyz,scxyz->oc",
                cotangent,
                tap_slice(padded, tap_offsets(tap_index), extent),
                preferred_element_type=jnp.float32,
            )
            for tap_index in range(27)
        ]
    )


def pad_dims(values, widths):
    return jnp.pad(values, ((0, 0), (0, 0)) + widths)


def avg_pool(values):
    shape_in = values.shape
    blocks = values.reshape(
        shape_in[0], shape_in[1], shape_in[2] // 2, 2, shape_in[3] // 2, 2, shape_in[4] // 2, 2
    )
    return jnp.sum(blocks, axis=(3, 5, 7)) * 0.125


def spread_up(values):
    small = values.shape
    grown = jnp.broadcast_to(
        values.reshape(small[0], small[1], small[2], 1, small[3], 1, small[4], 1),
        (small[0], small[1], small[2], 2, small[3], 2, small[4], 2),
    )
    return grown.reshape(small[0], small[1], 2 * small[2], 2 * small[3], 2 * small[4]) * 0.125


def on_device(samples, early_filters, deep_filters, deep_cotangent):
    extent_early = samples.shape[2:]
    bordered = with_halo(samples, (("space", 2), ("chan", 3)), 1)
    bordered = pad_dims(bordered, ((0, 0), (0, 0), (1, 1)))
    pre_early = forward_conv(bordered, early_filters, extent_early)
    pooled = avg_pool(jax.nn.silu(pre_early)).astype(jnp.bfloat16)
    slab = lax.all_gather(pooled, "chan", axis=3, tiled=True)
    extent_deep = slab.shape[2:]
    slab_padded = with_halo(slab, (("space", 2),), 1)
    slab_padded = pad_dims(slab_padded, ((0, 0), (1, 1), (1, 1)))
    pre_deep = forward_conv(slab_padded, deep_filters, extent_deep)
    deep_act = jax.nn.silu(pre_deep).astype(jnp.bfloat16)
    deep_in = (deep_cotangent.astype(jnp.float32) * slope(pre_deep)).astype(jnp.bfloat16)
    deep_share = filter_grad(deep_in, slab_padded, extent_deep)
    back_padded = with_halo(deep_in, (("space", 2),), 1)
    back_padded = pad_dims(back_padded, ((0, 0), (1, 1), (1, 1)))
    pooled_terms = backward_conv(back_padded, deep_filters, extent_deep)
    pooled_grad = lax.psum_scatter(pooled_terms, "chan", scatter_dimension=3, tiled=True)
    deep_grad = lax.psum(deep_share, ("dp", "space"))
    early_in = (spread_up(pooled_grad) * slope(pre_early)).astype(jnp.bfloat16)
    early_grad = lax.psum(filter_grad(early_in, bordered, extent_early), ("dp", "space", "chan"))
    return (deep_act, deep_grad, early_grad)


def solution(mesh):
    placed = (
        P("dp", None, "space", "chan", None),
        P(),
        P(None, "chan", None),
        P("dp", "chan", "space", None, None),
    )
    return jax.shard_map(
        on_device,
        mesh=mesh,
        in_specs=placed,
        out_specs=(P("dp", "chan", "space", None, None), P(None, "chan", None), P()),
        check_vma=False,
    )
```

profile of v0, /device:TPU:1, one launch (start us, length us, event | category | flops | bytes accessed | tf_op | source)
XLA Modules:
  0.0 637.5 jit_solution(10839379370725791738)
XLA Ops:
  9.2 6.2 collective-permute-start
  17.4 3.0 fusion.332
  20.9 3.7 collective-permute-done.1
  24.7 3.6 collective-permute-start.2
  29.5 2.8 fusion.335
  32.3 2.8 fusion.338
  37.4 2.8 fusion.302
  40.3 3.1 fusion.303
  46.1 3.1 fusion.305
  52.0 3.1 fusion.307
  55.1 2.8 fusion.308
  57.9 3.1 fusion.309
  63.8 3.1 fusion.311
  66.9 2.8 fusion.312
  69.8 3.1 fusion.313
  72.9 2.8 fusion.314
  75.7 3.2 fusion.315
  78.8 3.1 fusion.316
  82.0 3.1 fusion.317
  96.0 2.8 fusion.433
  101.5 2.8 fusion.410
  104.4 37.3 %fusion.10 = (f32[1,128,4,8,256]{1,4,3,2,0:T(8,128)}, f32[1,128,4,8,256]{1,4,3,2,0:T(8,128)}) fusion(bf16[27,128,64]{1,2,0:T(8,128)(2,1)S(1)} %copy-done.24, bf16[1,64,6,10,258]{4,1,3,2,0:T(8,128)(2,1)S(1)} %fusion.15, f32[4,8,256,128]{3,2,1,0:T(8,128)} %fusion.410, f32[4,8,256,128]{3,2,1,0:T(8,128)} %fusion.318, f32[4,8,256,128]{3,2,1,0:T(8,128)} %fusion.317, ...), kind=kOutput, calls=%fused_computation.35 | convolution fusion | flops 165675008 | bytes 118505472 | tf_op jit(solution)/shard_map/oc,scxyz->soxyz/dot_general | solution.py:42
  141.7 4.7 reduce_sum.9
  149.3 25.1 %all-gather.3.cloned.1.call-done = bf16[128,2,16,128]{3,0,2,1:T(8,128)(2,1)} async-done(((bf16[128,2,4,128]{3,0,2,1:T(8,128)(2,1)}), bf16[128,2,16,128]{3,0,2,1:T(8,128)(2,1)}) %all-gather.3.cloned.1.call-update) | async-done | bytes 1048592 | tf_op jit(solution)/shard_map/all_gather | solution.py:107
  176.6 6.1 collective-permute-start.4
  187.5 7.3 %collective-permute-done.4 = bf16[1,128,1,16,128]{4,1,3,2,0:T(8,128)(2,1)} collective-permute-done((bf16[1,128,1,16,128]{4,1,3,2,0:T(8,128)(2,1)}, bf16[1,128,1,16,128]{4,1,3,2,0:T(8,128)(2,1)}, u32[]{:S(2)}, u32[]{:S(2)}) %collective-permute-start.4) | collective-permute-done | bytes 524320 | tf_op jit(solution)/shard_map/ppermute | solution.py:14
  195.0 5.4 select_maximum_fusion
  219.7 5.7 collective-permute-start.6
  286.7 20.6 %bitcast_add_fusion.11 = f32[1,128,2,16,128]{1,4,3,2,0:T(8,128)} fusion(f32[2,16,128,128]{3,2,1,0:T(8,128)} %fusion.340, f32[2,16,128,128]{3,2,1,0:T(8,128)} %fusion.341, f32[2,16,128,128]{3,2,1,0:T(8,128)} %fusion.342, f32[2,16,128,128]{3,2,1,0:T(8,128)} %fusion.344, f32[2,16,128,128]{3,2,1,0:T(8,128)} %fusion.347, f32[2,16,128,128]{3,2,1,0:T(8,128)} %fusion.348, ...), kind=kOutput, calls=%fused_computation.50 | convolution fusion | flops 80740352 | bytes 57163776 | tf_op jit(solution)/shard_map/oc,soxyz->scxyz/dot_general | solution.py:56
  329.6 36.8 %all-reduce.12.cloned.1.call-done = f32[1,128,2,16,128]{1,4,3,2,0:T(8,128)} async-done(((f32[1,128,2,16,128]{1,4,3,2,0:T(8,128)}), f32[1,128,2,16,128]{1,4,3,2,0:T(8,128)}) %all-reduce.12.cloned.1.call-update) | async-done | bytes 2097168
  404.7 69.4 %all-reduce.8.cloned.1.call-done = f32[27,64,128]{2,1,0:T(8,128)} async-done(((f32[27,64,128]{2,1,0:T(8,128)}), f32[27,64,128]{2,1,0:T(8,128)}) %all-reduce.8.cloned.1.call-update) | async-done | bytes 884752 | tf_op jit(solution)/shard_map/psum | solution.py:119
  474.0 152.3 %all-reduce.10.cloned.1.call-done = f32[27,128,64]{1,2,0:T(8,128)} async-done(((f32[27,128,64]{1,2,0:T(8,128)}), f32[27,128,64]{1,2,0:T(8,128)}) %all-reduce.10.cloned.1.call-update) | async-done | bytes 884752 | tf_op jit(solution)/shard_map/psum | solution.py:121
  (206 shorter events, 184.5 us)
Async XLA Ops:
  7.2 10.2 %copy-start.9 = (bf16[1,64,4,8,256]{4,3,2,1,0:T(8,128)(2,1)S(1)}, bf16[1,64,4,8,256]{4,3,2,1,0:T(8,128)(2,1)}, u32[]{:S(2)}) copy-start(bf16[1,64,4,8,256]{4,3,2,1,0:T(8,128)(2,1)} %param.4) | copy-start | bytes 3145732
  7.2 10.2 %copy-start.24 = (bf16[27,128,64]{1,2,0:T(8,128)(2,1)S(1)}, bf16[27,128,64]{1,2,0:T(8,128)(2,1)}, u32[]{:S(2)}) copy-start(bf16[27,128,64]{1,2,0:T(8,128)(2,1)} %param.5) | copy-start | bytes 1327108
  7.2 167.2 %all-gather.3.cloned.1.call-start = ((), (), s32[]{:S(2)}) async-start(), calls=%async_computation.2 | async-start | bytes 1310720 | tf_op jit(solution)/shard_map/all_gather | solution.py:107
  9.1 23.2 %copy-start.6 = (bf16[1,64,4,8,256]{4,1,3,2,0:T(8,128)(2,1)}, bf16[1,64,4,8,256]{4,1,3,2,0:T(8,128)(2,1)S(1)}, u32[]{:S(2)}) copy-start(bf16[1,64,4,8,256]{4,1,3,2,0:T(8,128)(2,1)S(1)} %copy.43) | copy-start | bytes 3145732
  9.2 11.1 %collective-permute-start = (bf16[1,64,1,8,256]{4,1,3,2,0:T(8,128)(2,1)S(1)}, bf16[1,64,1,8,256]{4,1,3,2,0:T(8,128)(2,1)S(1)}, u32[]{:S(2)}, u32[]{:S(2)}) collective-permute-start(bf16[1,64,1,8,256]{4,1,3,2,0:T(8,128)(2,1)S(1)} %get-tuple-element.16), channel_id=1, source_target_pairs={{0,4},{4,8},{8,12},{12,16},{16,20},{20,24},{24,28},{28,32},{32,36}... | collective-permute-start | bytes 786440 | tf_op jit(solution)/shard_map/ppermute | solution.py:14
  15.4 9.2 %collective-permute-start.1 = (bf16[1,64,1,8,256]{4,1,3,2,0:T(8,128)(2,1)S(1)}, bf16[1,64,1,8,256]{4,1,3,2,0:T(8,128)(2,1)S(1)}, u32[]{:S(2)}, u32[]{:S(2)}) collective-permute-start(bf16[1,64,1,8,256]{4,1,3,2,0:T(8,128)(2,1)S(1)} %get-tuple-element.15), channel_id=1, source_target_pairs={{4,0},{8,4},{12,8},{16,12},{20,16},{24,20},{28,24},{32,28},{36,32}... | collective-permute-start | bytes 786440 | tf_op jit(solution)/shard_map/ppermute | solution.py:15
  20.3 12.0 %copy-start.19 = (bf16[1,64,1,8,256]{4,1,3,2,0:T(8,128)(2,1)}, bf16[1,64,1,8,256]{4,1,3,2,0:T(8,128)(2,1)S(1)}, u32[]{:S(2)}) copy-start(bf16[1,64,1,8,256]{4,1,3,2,0:T(8,128)(2,1)S(1)} %collective-permute-done) | copy-start | bytes 786436
  24.6 7.7 %copy-start.17 = (bf16[1,64,1,8,256]{4,1,3,2,0:T(8,128)(2,1)}, bf16[1,64,1,8,256]{4,1,3,2,0:T(8,128)(2,1)S(1)}, u32[]{:S(2)}) copy-start(bf16[1,64,1,8,256]{4,1,3,2,0:T(8,128)(2,1)S(1)} %collective-permute-done.1) | copy-start | bytes 786436
  24.6 76.9 %copy-start.1 = (bf16[1,64,6,8,256]{4,1,3,2,0:T(8,128)(2,1)}, bf16[1,64,6,8,256]{4,1,3,2,0:T(8,128)(2,1)S(1)}, u32[]{:S(2)}) copy-start(bf16[1,64,6,8,256]{4,1,3,2,0:T(8,128)(2,1)S(1)} %constant_dynamic-update-slice_fusion) | copy-start | bytes 4718596
  24.7 10.5 %collective-permute-start.2 = (bf16[1,64,6,1,256]{4,1,3,2,0:T(8,128)(2,1)S(1)}, bf16[1,64,6,1,256]{4,1,3,2,0:T(8,128)(2,1)S(1)}, u32[]{:S(2)}, u32[]{:S(2)}) collective-permute-start(bf16[1,64,6,1,256]{4,1,3,2,0:T(8,128)(2,1)S(1)} %get-tuple-element.9), channel_id=1, source_target_pairs={{0,1},{1,2},{2,3},{4,5},{5,6},{6,7},{8,9},{9,10},{10,11},{12,13},{... | collective-permute-start | bytes 589832 | tf_op jit(solution)/shard_map/ppermute | solution.py:14
  28.2 6.9 %collective-permute-start.3 = (bf16[1,64,6,1,256]{4,1,3,2,0:T(8,128)(2,1)S(1)}, bf16[1,64,6,1,256]{4,1,3,2,0:T(8,128)(2,1)S(1)}, u32[]{:S(2)}, u32[]{:S(2)}) collective-permute-start(bf16[1,64,6,1,256]{4,1,3,2,0:T(8,128)(2,1)S(1)} %get-tuple-element.10), channel_id=1, source_target_pairs={{1,0},{2,1},{3,2},{5,4},{6,5},{7,6},{9,8},{10,9},{11,10},{13,12},{... | collective-permute-start | bytes 589832 | tf_op jit(solution)/shard_map/ppermute | solution.py:15
  35.2 63.6 %copy-start.13 = (bf16[1,64,6,1,256]{4,1,3,2,0:T(8,128)(2,1)}, bf16[1,64,6,1,256]{4,1,3,2,0:T(8,128)(2,1)S(1)}, u32[]{:S(2)}) copy-start(bf16[1,64,6,1,256]{4,1,3,2,0:T(8,128)(2,1)S(1)} %collective-permute-done.2) | copy-start | bytes 589828
  35.2 66.4 %copy-start.11 = (bf16[1,64,6,1,256]{4,1,3,2,0:T(8,128)(2,1)}, bf16[1,64,6,1,256]{4,1,3,2,0:T(8,128)(2,1)S(1)}, u32[]{:S(2)}) copy-start(bf16[1,64,6,1,256]{4,1,3,2,0:T(8,128)(2,1)S(1)} %collective-permute-done.3) | copy-start | bytes 589828
  146.4 38.3 %copy-start.26 = (u32[128]{0:T(128)S(1)}, u32[128]{0:T(128)}, u32[]{:S(2)}) copy-start(u32[128]{0:T(128)} %constant.25) | copy-start | bytes 1540
  149.2 217.2 %all-reduce.12.cloned.1.call-start = ((), (), s32[]{:S(2)}) async-start(), calls=%async_computation.3 | async-start | bytes 4194304
  176.6 18.1 %collective-permute-start.4 = (bf16[1,128,1,16,128]{4,1,3,2,0:T(8,128)(2,1)}, bf16[1,128,1,16,128]{4,1,3,2,0:T(8,128)(2,1)}, u32[]{:S(2)}, u32[]{:S(2)}) collective-permute-start(bf16[1,128,1,16,128]{4,1,3,2,0:T(8,128)(2,1)} %get-tuple-element.13), channel_id=1, source_target_pairs={{0,4},{4,8},{8,12},{12,16},{16,20},{20,24},{24,28},{28,32},{32,36}... | collective-permute-start | bytes 1572872 | tf_op jit(solution)/shard_map/ppermute | solution.py:14
  182.7 12.2 %collective-permute-start.5 = (bf16[1,128,1,16,128]{4,1,3,2,0:T(8,128)(2,1)}, bf16[1,128,1,16,128]{4,1,3,2,0:T(8,128)(2,1)S(1)}, u32[]{:S(2)}, u32[]{:S(2)}) collective-permute-start(bf16[1,128,1,16,128]{4,1,3,2,0:T(8,128)(2,1)} %get-tuple-element.14), channel_id=1, source_target_pairs={{4,0},{8,4},{12,8},{16,12},{20,16},{24,20},{28,24},{32,28},{36,32}... | collective-permute-start | bytes 1572872 | tf_op jit(solution)/shard_map/ppermute | solution.py:15
  187.5 12.9 %copy-start.21 = (bf16[27,64,128]{2,1,0:T(8,128)(2,1)S(1)}, bf16[27,64,128]{2,1,0:T(8,128)(2,1)}, u32[]{:S(2)}) copy-start(bf16[27,64,128]{2,1,0:T(8,128)(2,1)} %param.6) | copy-start | bytes 1327108
  195.0 16.7 %copy-start.15 = (bf16[1,128,1,16,128]{4,1,3,2,0:T(8,128)(2,1)}, bf16[1,128,1,16,128]{4,1,3,2,0:T(8,128)(2,1)S(1)}, u32[]{:S(2)}) copy-start(bf16[1,128,1,16,128]{4,1,3,2,0:T(8,128)(2,1)S(1)} %collective-permute-done.5) | copy-start | bytes 1572868
  200.3 34.4 %copy-start = (bf16[1,128,4,18,130]{4,1,3,2,0:T(8,128)(2,1)}, bf16[1,128,4,18,130]{4,1,3,2,0:T(8,128)(2,1)S(1)}, u32[]{:S(2)}) copy-start(bf16[1,128,4,18,130]{4,1,3,2,0:T(8,128)(2,1)S(1)} %select_maximum_fusion) | copy-start | bytes 7188484
  217.7 17.5 %collective-permute-start.7 = (bf16[1,64,1,16,128]{4,1,3,2,0:T(8,128)(2,1)S(1)}, bf16[1,64,1,16,128]{4,1,3,2,0:T(8,128)(2,1)S(1)}, u32[]{:S(2)}, u32[]{:S(2)}) collective-permute-start(bf16[1,64,1,16,128]{4,1,3,2,0:T(8,128)(2,1)S(1)} %get-tuple-element.18), channel_id=1, source_target_pairs={{4,0},{8,4},{12,8},{16,12},{20,16},{24,20},{28,24},{32,28},{36,32}... | collective-permute-start | bytes 786440 | tf_op jit(solution)/shard_map/ppermute | solution.py:15
  219.7 16.5 %collective-permute-start.6 = (bf16[1,64,1,16,128]{4,1,3,2,0:T(8,128)(2,1)S(1)}, bf16[1,64,1,16,128]{4,1,3,2,0:T(8,128)(2,1)S(1)}, u32[]{:S(2)}, u32[]{:S(2)}) collective-permute-start(bf16[1,64,1,16,128]{4,1,3,2,0:T(8,128)(2,1)S(1)} %get-tuple-element.17), channel_id=1, source_target_pairs={{0,4},{4,8},{8,12},{12,16},{16,20},{20,24},{24,28},{28,32},{32,36}... | collective-permute-start | bytes 786440 | tf_op jit(solution)/shard_map/ppermute | solution.py:14
  238.0 42.9 %copy-start.3 = (bf16[1,64,4,18,130]{4,1,3,2,0:T(8,128)(2,1)}, bf16[1,64,4,18,130]{4,1,3,2,0:T(8,128)(2,1)S(1)}, u32[]{:S(2)}) copy-start(bf16[1,64,4,18,130]{4,1,3,2,0:T(8,128)(2,1)S(1)} %select_maximum_fusion.2) | copy-start | bytes 3594244
  307.4 166.6 %all-reduce.8.cloned.1.call-start = ((), (), s32[]{:S(2)}) async-start(), calls=%async_computation | async-start | bytes 1769472 | tf_op jit(solution)/shard_map/psum | solution.py:119
  307.4 10.4 %copy-start.5 = (bf16[128,2,16,128]{3,0,2,1:T(8,128)(2,1)S(1)}, bf16[128,2,16,128]{3,0,2,1:T(8,128)(2,1)}, u32[]{:S(2)}) copy-start(bf16[128,2,16,128]{3,0,2,1:T(8,128)(2,1)} %all-gather.3.cloned.1.call-done) | copy-start | bytes 3145732
  307.4 10.4 %copy-start.16 = (bf16[1,128,1,16,128]{4,1,3,2,0:T(8,128)(2,1)S(1)}, bf16[1,128,1,16,128]{4,1,3,2,0:T(8,128)(2,1)}, u32[]{:S(2)}) copy-start(bf16[1,128,1,16,128]{4,1,3,2,0:T(8,128)(2,1)} %copy-done.15) | copy-start | bytes 1572868
  329.6 296.8 %all-reduce.10.cloned.1.call-start = ((), (), s32[]{:S(2)}) async-start(), calls=%async_computation.1 | async-start | bytes 1769472 | tf_op jit(solution)/shard_map/psum | solution.py:121
  366.4 3.2 copy-start.8
  373.8 2.3 copy-start.7
  373.8 2.3 copy-start.20
  384.3 2.3 copy-start.10
  395.3 2.3 copy-start.18
  (7 other events, 9.5 us)
Sparse Core Ops, SparseCore 0:
  149.4 24.9 all-gather.2
  307.5 58.8 all-reduce.11
  370.6 103.3 all-reduce.7
  480.0 146.3 all-reduce.9
where the time goes:
time: 643 us; the launch traced here: 637 us
  waiting for transfers between devices  295 us (46%)
  matrix products  265 us (41%)
  starting transfers between devices  28.8 us (4%)
  other arithmetic  18.7 us (3%)
  local copies, waits for them, and re-layouts  15.4 us (2%)
  between operations  15.3 us (2%)
    psum x1, waiting for transfers between devices, on_device(): lax.psum(filter_grad(early_in, bordered, extent_early), ('dp', 'space', '...  152 us
    dot_general x54, matrix products, forward_conv(): jnp.einsum('oc,scxyz->soxyz', filters[tap_index], tap_slice(padded, tap_o...  129 us
    dot_general x27, matrix products, backward_conv(): jnp.einsum('oc,soxyz->scxyz', filters[tap_index], tap_slice(padded, start...  71.2 us
    psum x1, waiting for transfers between devices, on_device(): deep_grad = lax.psum(deep_share, ('dp', 'space'))  69.4 us
    dot_general x54, matrix products, filter_grad(): jnp.einsum('soxyz,scxyz->oc', cotangent, tap_slice(padded, tap_offsets(ta...  64.3 us
    unnamed x5, waiting for transfers between devices  36.9 us
    all_gather x1, waiting for transfers between devices, on_device(): slab = lax.all_gather(pooled, 'chan', axis=3, tiled=True)  25.1 us
    ppermute x4, starting transfers between devices, with_halo(): before = lax.ppermute(last, axis, up)  21.6 us
  transfers between devices with their start and end apart: 12, of which 7 were waited for; matrix products, arithmetic and copies ran while one was open for 13% of the time, Pallas kernels for 0%

commit v1 on v0

v1 whole, which is shorter than its diff:
```python
import jax
import jax.numpy as jnp
from jax import lax
from jax.experimental import pallas as pl
from jax.experimental.pallas import tpu as pltpu
from jax.sharding import PartitionSpec as P

BF16 = jnp.bfloat16
F32 = jnp.float32
MESH = pl.DeviceIdType.MESH

SIDES = [(dx, dy) for dx in (-1, 0, 1) for dy in (-1, 0, 1) if (dx, dy) != (0, 0)]


def dot(a, b):
    return lax.dot_general(a, b, (((1,), (0,)), ((), ())), preferred_element_type=F32)


def dot_nt(a, b):
    return lax.dot_general(a, b, (((1,), (1,)), ((), ())), preferred_element_type=F32)


def selector(rows, cols, hit):
    row = lax.broadcasted_iota(jnp.int32, (rows, cols), 0)
    col = lax.broadcasted_iota(jnp.int32, (rows, cols), 1)
    return jnp.where(hit(row, col), 1.0, 0.0).astype(BF16)


def sigmoid(u):
    return 0.5 + 0.5 * jnp.tanh(0.5 * u)


def sent_and_landed(side, length):
    if side == 0:
        return (1, length), (1, length)
    if side == 1:
        return (length, 1), (0, 1)
    return (1, 1), (length + 1, 1)


def build_early_weights(ef, w9):
    places = [selector(64, 256, lambda r, c, s=s: c == r + 64 * s) for s in range(4)]

    def body(ae, carry):
        for p in range(2):
            w9[ae, p * 128 : (p + 1) * 128, :] = sum(dot(ef[3 * ae + f], places[f + p]) for f in range(3)).astype(BF16)
        return carry

    lax.fori_loop(0, 9, body, 0)


def place_taps(block, spread, taps_in, x, first_y, count):
    wide = dot(block, spread[...]).astype(BF16)
    for y in range(count):
        for s in range(4):
            taps_in[x, s * 64 : (s + 1) * 64, pl.ds((first_y + y) * 128, 128)] = wide[
                y * 64 : (y + 1) * 64, s * 128 : (s + 1) * 128
            ]


def early_forward(taps_in, w9, slopes, pooled):
    def body(i, carry):
        X, Y = i // 4, i % 4
        total = None
        for dx in range(2):
            x = 2 * X + dx
            pre = None
            for a in range(3):
                for e in range(3):
                    lanes = pl.ds(pl.multiple_of((2 * Y + e) * 128, 128), 256)
                    term = dot(w9[3 * a + e], taps_in[x + a, :, lanes])
                    pre = term if pre is None else pre + term
            s = sigmoid(pre)
            slopes[x, :, pl.ds(pl.multiple_of(Y * 256, 256), 256)] = s * (1.0 + pre * (1.0 - s))
            act = pre * s
            act = act[:128] + act[128:]
            act = act[:, :128] + act[:, 128:]
            total = act if total is None else total + act
        pooled[X + 1, 128:256, pl.ds(pl.multiple_of((Y + 1) * 128, 128), 128)] = (total * 0.125).astype(BF16)
        return carry

    lax.fori_loop(0, 8, body, 0)


def shift_pooled(pooled):
    shifts = selector(128, 256, lambda r, c: r == jnp.where(c < 128, c - 1, c - 127))

    def body(i, carry):
        x = i // 6
        lanes = pl.ds(pl.multiple_of((i % 6) * 128, 128), 128)
        both = dot(pooled[x, 128:256, lanes], shifts).astype(BF16)
        pooled[x, 0:128, lanes] = both[:, :128]
        pooled[x, 256:384, lanes] = both[:, 128:]
        return carry

    lax.fori_loop(0, 24, body, 0)


def transpose_deep_weights(wd, wdt):
    eye = selector(128, 128, lambda r, c: r == c)

    def body(ae, carry):
        for f in range(3):
            wdt[ae, f * 128 : (f + 1) * 128, :] = dot_nt(eye, wd[ae, :, f * 128 : (f + 1) * 128]).astype(BF16)
        return carry

    lax.fori_loop(0, 9, body, 0)


def deep_forward(pooled, wd, ct, act_out, deep_in):
    def body(i, carry):
        X, h = i // 2, i % 2
        pre = None
        for a in range(3):
            for e in range(3):
                lanes = pl.ds(pl.multiple_of(h * 256 + e * 128, 128), 256)
                term = dot(wd[3 * a + e], pooled[X + a, :, lanes])
                pre = term if pre is None else pre + term
        s = sigmoid(pre)
        own = pl.ds(pl.multiple_of(h * 256, 256), 256)
        act_out[X, :, own] = (pre * s).astype(BF16)
        slope = s * (1.0 + pre * (1.0 - s))
        lanes = pl.ds(pl.multiple_of(h * 256 + 128, 128), 256)
        deep_in[X + 1, :, lanes] = (ct[X, :, own].astype(F32) * slope).astype(BF16)
        return carry

    lax.fori_loop(0, 4, body, 0)


def deep_gradient(deep_in, pooled, out):
    def body(i, carry):
        a, e = i // 3, i % 3
        lanes = pl.ds(pl.multiple_of(e * 128, 128), 512)
        total = None
        for X in range(2):
            term = dot_nt(deep_in[X + 1, :, 128:640], pooled[X + a, :, lanes])
            total = term if total is None else total + term
        out[i] = total.astype(BF16)
        return carry

    lax.fori_loop(0, 9, body, 0)


def early_cotangent(deep_in, wdt, slopes, early_in):
    column = lax.broadcasted_iota(jnp.int32, (128, 128), 1)

    def body(i, carry):
        X, h = i // 2, i % 2
        total = None
        for a in range(3):
            for e in range(3):
                lanes = pl.ds(pl.multiple_of(h * 256 + (2 - e) * 128, 128), 256)
                term = dot(wdt[3 * a + e], deep_in[X + 2 - a, :, lanes])
                total = term if total is None else total + term
        for k in range(2):
            part = total[:, k * 128 : (k + 1) * 128]
            grad = part[128:256]
            grad += jnp.where(column < 127, pltpu.roll(part[0:128], 127, 1), 0.0)
            grad += jnp.where(column > 0, pltpu.roll(part[256:384], 1, 1), 0.0)
            grad *= 0.125
            for dx in range(2):
                for dy in range(2):
                    lanes = pl.ds(pl.multiple_of((4 * h + 2 * k + dy) * 128, 128), 128)
                    for p in range(2):
                        rows = slice(p * 128, (p + 1) * 128)
                        early_in[2 * X + dx, rows, lanes] = (grad * slopes[2 * X + dx, rows, lanes]).astype(BF16)
        return carry

    lax.fori_loop(0, 4, body, 0)


def early_gradient(early_in, taps_in, out):
    def body(i, carry):
        a, e = i // 3, i % 3
        lanes = pl.ds(pl.multiple_of(e * 128, 128), 1024)
        total = None
        for x in range(4):
            term = dot_nt(early_in[x], taps_in[x + a, :, lanes])
            total = term if total is None else total + term
        out[i] = (total[:128] + pltpu.roll(total[128:], 192, 1)).astype(BF16)
        return carry

    lax.fori_loop(0, 9, body, 0)


def kernel(
    samples, ef, wd_own, ct_own,
    act_out, dg_out, eg_out,
    sample_ext, taps_in, w9, spread, slopes, pooled, wd, wdt, ct, act, deep_in, early_in,
    dg, dg_a, dg_s, dg_b, dg_full, eg, eg_a, eg_s, eg_b, eg_full,
    halo_send, halo_recv, chan_send, chan_recv, a_send, a_recv, b_send, b_recv,
):
    dp, space, chan = lax.axis_index("dp"), lax.axis_index("space"), lax.axis_index("chan")
    core, chip_row = space % 2, space // 2
    rank_a = chan * 2 + core
    rank_b = chip_row * 2 + dp

    def side_device(dx, dy):
        return {"dp": dp, "space": (space + dx + 16) % 16, "chan": (chan + dy + 4) % 4}

    def chan_device(j):
        return {"dp": dp, "space": space, "chan": (chan + j) % 4}

    def a_device(j):
        r = (rank_a + j) % 8
        return {"dp": dp, "space": chip_row * 2 + r % 2, "chan": r // 2}

    def b_device(j):
        r = (rank_b + j) % 16
        return {"dp": r % 2, "space": (r // 2) * 2 + core, "chan": chan}

    barrier = pltpu.get_barrier_semaphore()
    peers = [side_device(dx, dy) for dx, dy in SIDES]
    peers += [a_device(j) for j in range(1, 8)] + [b_device(j) for j in range(1, 16)]
    for peer in peers:
        pl.semaphore_signal(barrier, inc=1, device_id=peer, device_id_type=MESH)

    build_early_weights(ef, w9)
    spread[...] = selector(256, 512, lambda r, c: r == 2 * (c % 128) + c // 128 - 1)

    pl.semaphore_wait(barrier, len(peers))

    sends = []

    def remote(src, dst, send_sem, recv_sem, device):
        copy = pltpu.make_async_remote_copy(
            src_ref=src, dst_ref=dst, send_sem=send_sem, recv_sem=recv_sem, device_id=device, device_id_type=MESH
        )
        copy.start()
        sends.append(copy)
        return copy

    def halo(n, view):
        copies = []
        for k, (dx, dy) in enumerate(SIDES):
            src, dst = view(dx, dy)
            copies.append(remote(src, dst, halo_send.at[n, k], halo_recv.at[n, k], side_device(dx, dy)))
        return copies

    def sample_view(dx, dy):
        (sx, nx), (tx, _) = sent_and_landed(dx, 4)
        (sy, ny), (ty, _) = sent_and_landed(dy, 8)
        src = samples.at[pl.ds(sx - 1, nx), pl.ds(sy - 1, ny)]
        return src, sample_ext.at[pl.ds(tx, nx), pl.ds(ty, ny)]

    def field_view(ref, first, rows):
        def view(dx, dy):
            (sx, nx), (tx, _) = sent_and_landed(dx, 2)
            (sy, ny), (ty, _) = sent_and_landed(dy, 4)
            block = pl.ds(first, rows)
            src = ref.at[pl.ds(sx, nx), block, pl.ds(sy * 128, ny * 128)]
            return src, ref.at[pl.ds(tx, nx), block, pl.ds(ty * 128, ny * 128)]

        return view

    def clear_outside(ref, rows, lanes):
        last, width = ref.shape[0] - 1, ref.shape[2]

        def clear(x, span):
            ref[x, rows, span] = jnp.zeros((rows.stop - rows.start, span.stop - span.start), BF16)

        @pl.when(space == 0)
        def _():
            clear(0, slice(0, width))

        @pl.when(space == 15)
        def _():
            clear(last, slice(0, width))

        @pl.when(chan == 0)
        def _():
            for x in range(last + 1):
                clear(x, slice(0, lanes))

        @pl.when(chan == 3)
        def _():
            for x in range(last + 1):
                clear(x, slice(width - lanes, width))

    sample_halo = halo(0, sample_view)
    wd_copies, ct_copies = [], []
    mine = pl.ds(pl.multiple_of(chan * 64, 64), 64)
    for j in (1, 2, 3):
        wd_copies.append(remote(wd_own, wd.at[:, mine, :], chan_send.at[0, j], chan_recv.at[0, j], chan_device(j)))
    for j in (1, 2, 3):
        theirs = pl.ds(pl.multiple_of((chan + j) % 4 * 512, 512), 512)
        ct_copies.append(
            remote(ct_own.at[:, :, theirs], ct.at[:, mine, :], chan_send.at[1, j], chan_recv.at[1, j], chan_device(j))
        )
    wd[:, mine, :] = wd_own[...]
    ct[:, mine, :] = ct_own[:, :, pl.ds(pl.multiple_of(chan * 512, 512), 512)]

    for x in range(4):
        place_taps(samples[x].reshape(512, 256), spread, taps_in, x + 1, 1, 8)
    for copy in sample_halo:
        copy.wait_recv()
    for x in (0, 5):
        place_taps(sample_ext[x].reshape(640, 256), spread, taps_in, x, 0, 10)
    for y in (0, 9):
        for x in range(1, 5):
            place_taps(sample_ext[x, y], spread, taps_in, x, y, 1)
    clear_outside(taps_in, slice(0, 256), 128)

    early_forward(taps_in, w9, slopes, pooled)
    pooled_halo = halo(1, field_view(pooled, 128, 128))
    for copy in wd_copies + ct_copies:
        copy.wait_recv()
    transpose_deep_weights(wd, wdt)
    for copy in pooled_halo:
        copy.wait_recv()
    clear_outside(pooled, slice(128, 256), 128)
    shift_pooled(pooled)

    deep_forward(pooled, wd, ct, act, deep_in)
    deep_halo = halo(2, field_view(deep_in, 0, 256))
    act_copies = []
    here = pl.ds(pl.multiple_of(chan * 512, 512), 512)
    for j in (1, 2, 3):
        theirs = pl.ds(pl.multiple_of((chan + j) % 4 * 64, 64), 64)
        act_copies.append(
            remote(act.at[:, theirs, :], act_out.at[:, :, here], chan_send.at[2, j], chan_recv.at[2, j], chan_device(j))
        )
    act_out[:, :, here] = act[:, mine, :]

    deep_gradient(deep_in, pooled, dg)

    def reduce_a(n, src, dst, rows):
        copies = []
        for j in range(1, 8):
            theirs = pl.ds(pl.multiple_of((rank_a + j) % 8 * rows, rows), rows)
            copies.append(remote(src.at[:, theirs, :], dst.at[j], a_send.at[n, j], a_recv.at[n, j], a_device(j)))
        return copies

    def sum_a(src, dst, out, rows):
        own = pl.ds(pl.multiple_of(rank_a * rows, rows), rows)

        def body(ae, carry):
            total = src[ae, own, :].astype(F32)
            for j in range(1, 8):
                total += dst[j, ae].astype(F32)
            out[ae] = total.astype(BF16)
            return carry

        lax.fori_loop(0, 9, body, 0)

    conditional = []

    def remote_if(pred, src, dst, send_sem, recv_sem, device):
        copy = pltpu.make_async_remote_copy(
            src_ref=src, dst_ref=dst, send_sem=send_sem, recv_sem=recv_sem, device_id=device, device_id_type=MESH
        )

        @pl.when(pred)
        def _():
            copy.start()

        conditional.append((pred, copy))

    def reduce_b(n, src, dst):
        for j in range(1, 16):
            r = (rank_b + j) % 16
            row = jnp.minimum(r, 8)
            remote_if(r < 9, src.at[row], dst.at[j], b_send.at[n, j], b_recv.at[n, j], b_device(j))

    def sum_and_spread_b(n, src, dst, full, rows, first):
        own = pl.ds(first, rows)

        @pl.when(rank_b < 9)
        def _():
            total = src[rank_b].astype(F32)
            for j in range(1, 16):
                pltpu.make_async_remote_copy(
                    src_ref=src.at[0], dst_ref=dst.at[j], send_sem=b_send.at[n, j], recv_sem=b_recv.at[n, j],
                    device_id=b_device(j), device_id_type=MESH,
                ).wait_recv()
            for j in range(1, 16):
                total += dst[j].astype(F32)
            full[rank_b, own, :] = total.astype(BF16)

        block = full.at[jnp.minimum(rank_b, 8), own, :]
        for j in range(1, 16):
            remote_if(rank_b < 9, block, block, b_send.at[n + 2, j], b_recv.at[n + 2, j], b_device(j))

    def landed_b(n, full, rows, first):
        for j in range(1, 16):
            r = (rank_b - j + 16) % 16
            block = full.at[jnp.minimum(r, 8), pl.ds(first, rows), :]

            @pl.when(r < 9)
            def _():
                pltpu.make_async_remote_copy(
                    src_ref=block, dst_ref=block, send_sem=b_send.at[n + 2, j], recv_sem=b_recv.at[n + 2, j],
                    device_id=b_device(j), device_id_type=MESH,
                ).wait_recv()

    for copy in deep_halo:
        copy.wait_recv()
    dg_copies = reduce_a(0, dg, dg_a, 32)
    clear_outside(deep_in, slice(0, 256), 128)
    early_cotangent(deep_in, wdt, slopes, early_in)
    early_gradient(early_in, taps_in, eg)
    eg_copies = reduce_a(1, eg, eg_a, 16)

    for copy in dg_copies:
        copy.wait_recv()
    sum_a(dg, dg_a, dg_s, 32)
    reduce_b(0, dg_s, dg_b)
    for copy in eg_copies:
        copy.wait_recv()
    sum_a(eg, eg_a, eg_s, 16)
    reduce_b(1, eg_s, eg_b)
    dg_first = pl.multiple_of(core * 32, 32)
    eg_first = pl.multiple_of(rank_a * 16, 16)
    sum_and_spread_b(0, dg_s, dg_b, dg_full, 32, dg_first)
    sum_and_spread_b(1, eg_s, eg_b, eg_full, 16, eg_first)
    landed_b(0, dg_full, 32, dg_first)
    half = dg_full.at[:, pl.ds(dg_first, 32), :]
    sibling = {"dp": dp, "space": chip_row * 2 + 1 - core, "chan": chan}
    dg_pair = remote(half, half, a_send.at[2, 0], a_recv.at[2, 0], sibling)
    landed_b(1, eg_full, 16, eg_first)
    eg_last = []
    block = eg_full.at[:, pl.ds(eg_first, 16), :]
    for j in range(1, 8):
        eg_last.append(remote(block, block, a_send.at[2, j], a_recv.at[2, j], a_device(j)))

    other = dg_full.at[:, pl.ds(pl.multiple_of(32 - core * 32, 32), 32), :]
    pltpu.make_async_remote_copy(
        src_ref=half, dst_ref=other, send_sem=a_send.at[2, 0], recv_sem=a_recv.at[2, 0], device_id=sibling,
        device_id_type=MESH,
    ).wait_recv()
    for ae in range(9):
        for f in range(3):
            dg_out[3 * ae + f] = dg_full[ae, :, f * 128 : (f + 1) * 128].astype(F32)
    for j in range(1, 8):
        r = (rank_a - j + 8) % 8
        theirs = eg_full.at[:, pl.ds(pl.multiple_of(r * 16, 16), 16), :]
        pltpu.make_async_remote_copy(
            src_ref=block, dst_ref=theirs, send_sem=a_send.at[2, j], recv_sem=a_recv.at[2, j], device_id=a_device(j),
            device_id_type=MESH,
        ).wait_recv()
    for ae in range(9):
        for f in range(3):
            eg_out[3 * ae + f] = eg_full[ae, :, f * 64 : (f + 1) * 64].astype(F32)

    for copy in act_copies:
        copy.wait_recv()
    for copy in sends:
        copy.wait_send()
    for pred, copy in conditional:

        @pl.when(pred)
        def _():
            copy.wait_send()


def on_device(samples, early_filters, deep_filters, deep_cotangent):
    samples = samples[0].transpose(1, 2, 0, 3)
    deep_filters = deep_filters.reshape(9, 3, 64, 128).transpose(0, 2, 1, 3).reshape(9, 64, 384)
    deep_cotangent = deep_cotangent[0].transpose(1, 0, 2, 3).reshape(2, 64, 2048)
    act, deep_grad, early_grad = pl.pallas_call(
        kernel,
        out_shape=(
            jax.ShapeDtypeStruct((2, 64, 2048), BF16),
            jax.ShapeDtypeStruct((27, 64, 128), F32),
            jax.ShapeDtypeStruct((27, 128, 64), F32),
        ),
        in_specs=[pl.BlockSpec(memory_space=pltpu.VMEM)] * 4,
        out_specs=[pl.BlockSpec(memory_space=pltpu.VMEM)] * 3,
        scratch_shapes=[
            pltpu.VMEM((6, 10, 64, 256), BF16),
            pltpu.VMEM((6, 256, 1280), BF16),
            pltpu.VMEM((9, 256, 256), BF16),
            pltpu.VMEM((256, 512), BF16),
            pltpu.VMEM((4, 256, 1024), F32),
            pltpu.VMEM((4, 384, 768), BF16),
            pltpu.VMEM((9, 256, 384), BF16),
            pltpu.VMEM((9, 384, 256), BF16),
            pltpu.VMEM((2, 256, 512), BF16),
            pltpu.VMEM((2, 256, 512), BF16),
            pltpu.VMEM((4, 256, 768), BF16),
            pltpu.VMEM((4, 256, 1024), BF16),
            pltpu.VMEM((9, 256, 384), BF16),
            pltpu.VMEM((8, 9, 32, 384), BF16),
            pltpu.VMEM((9, 32, 384), BF16),
            pltpu.VMEM((16, 32, 384), BF16),
            pltpu.VMEM((9, 64, 384), BF16),
            pltpu.VMEM((9, 128, 256), BF16),
            pltpu.VMEM((8, 9, 16, 256), BF16),
            pltpu.VMEM((9, 16, 256), BF16),
            pltpu.VMEM((16, 16, 256), BF16),
            pltpu.VMEM((9, 128, 256), BF16),
            pltpu.SemaphoreType.DMA((3, 8)),
            pltpu.SemaphoreType.DMA((3, 8)),
            pltpu.SemaphoreType.DMA((3, 4)),
            pltpu.SemaphoreType.DMA((3, 4)),
            pltpu.SemaphoreType.DMA((3, 8)),
            pltpu.SemaphoreType.DMA((3, 8)),
            pltpu.SemaphoreType.DMA((4, 16)),
            pltpu.SemaphoreType.DMA((4, 16)),
        ],
        compiler_params=pltpu.CompilerParams(
            collective_id=0, has_side_effects=True, vmem_limit_bytes=56 * 1024 * 1024
        ),
        name="conv_step",
    )(samples, early_filters, deep_filters, deep_cotangent)
    act = act.reshape(2, 64, 16, 128).transpose(1, 0, 2, 3)[None]
    return act, deep_grad, early_grad


def solution(mesh):
    placed = (
        P("dp", None, "space", "chan", None),
        P(),
        P(None, "chan", None),
        P("dp", "chan", "space", None, None),
    )
    return jax.shard_map(
        on_device,
        mesh=mesh,
        in_specs=placed,
        out_specs=(P("dp", "chan", "space", None, None), P(None, "chan", None), P()),
        check_vma=False,
    )
```

time: 643 us -> 124 us (0.19)
  waiting for transfers between devices: 295 us -> 0 us
  matrix products: 265 us -> 0 us
  Pallas kernels: 0 us -> 112 us
  starting transfers between devices: 28.8 us -> 0 us
  other arithmetic: 18.7 us -> 0 us
  between operations: 15.3 us -> 0.69 us
    dot_general x135 -> x0, matrix products: 265 us -> none  [the longest x54 129 us: forward_conv(): jnp.einsum('oc,scxyz->soxyz', filters[tap_index], tap_slice(padded, tap_o...]
    psum x2 -> x0, waiting for transfers between devices: 222 us -> none  [the longest x1 152 us: on_device(): lax.psum(filter_grad(early_in, bordered, extent_early), ('dp', 'space', '...]
    pallas_call x0 -> x1, Pallas kernels: none -> 112 us  [on_device(): pl.pallas_call(kernel, out_shape=(jax.ShapeDtypeStruct((2, 64, 2048), BF1...]
    unnamed x5 -> x0, waiting for transfers between devices: 36.9 us -> none
    ppermute x8 -> x0, starting transfers between devices: 28.6 us -> none  [the longest x4 21.6 us: with_halo(): before = lax.ppermute(last, axis, up)]
    all_gather x1 -> x0, waiting for transfers between devices: 25.1 us -> none  [on_device(): slab = lax.all_gather(pooled, 'chan', axis=3, tiled=True)]
    ppermute x8 -> x0, waiting for transfers between devices: 11.2 us -> none  [the longest x4 7.31 us: with_halo(): before = lax.ppermute(last, axis, up)]
    concatenate x3 -> x0, other arithmetic: 9.44 us -> none  [with_halo(): value = jnp.concatenate([before, value, after], axis=dim)]
  transfers between devices with their start and end apart: 12 -> 0, of which waited for: 7 -> 0; matrix products, arithmetic and copies ran while one was open for 13% -> 0% of each run, Pallas kernels for 0% -> 0%
where the time goes in v1:
time: 124 us
  Pallas kernels  112 us (90%)
  local copies, waits for them, and re-layouts  11 us (9%)
    pallas_call x1, Pallas kernels, on_device(): pl.pallas_call(kernel, out_shape=(jax.ShapeDtypeStruct((2, 64, 2048), BF1...  112 us
    unnamed x15, local copies, waits for them, and re-layouts  6.45 us

profile of v1, /device:TPU:1, one launch (start us, length us, event | category | flops | bytes accessed | tf_op | source)
XLA Modules:
  0.0 124.0 jit_solution(13954570711098491817)
XLA Ops:
  0.6 0.0 copy-start.3
  0.6 1.2 reshape.22
  1.9 0.0 copy-start.4
  1.9 1.0 copy.19.ct_own
  2.8 0.0 copy-done.3
  2.8 0.0 copy-start.1
  2.8 0.4 copy.25
  3.2 1.1 reshape.19.wd_own
  4.4 0.0 copy-done.4
  4.4 1.2 copy.16.ef
  5.6 0.0 copy-done.1
  5.6 1.6 %copy.24 = bf16[1,64,4,8,256]{4,1,3,2,0:T(8,128)(2,1)} copy(bf16[1,64,4,8,256]{4,3,2,1,0:T(8,128)(2,1)S(1)} %copy-done.1) | data formatting | bytes 2097152 | tf_op args[0]
  7.2 112.4 %conv_step.1 = (bf16[2,64,2048]{2,1,0:T(8,128)(2,1)}, f32[27,64,128]{2,1,0:T(8,128)}, f32[27,128,64]{2,1,0:T(8,128)}) custom-call(bf16[4,8,64,256]{3,2,1,0:T(8,128)(2,1)} %bitcast.28, bf16[27,128,64]{2,1,0:T(8,128)(2,1)} %copy.16.ef, bf16[9,64,384]{2,1,0:T(8,128)(2,1)} %reshape.19.wd_own, bf16[2,64,2048]{2,1,0:T(8,128)(2,1)} %copy.19.ct_own), custom_call_target="tpu_custom_call" | custom-call | tf_op jit(solution)/shard_map/conv_step/pallas_call | solution.py:460
  119.5 0.0 copy-start
  119.5 1.3 %copy.20 = bf16[16,8,16,128]{3,2,1,0:T(8,128)(2,1)S(1)} copy(bf16[16,8,16,128]{3,1,2,0:T(8,128)(2,1)} %bitcast.32) | data formatting | bytes 1048576
  120.8 0.0 copy-start.2
  120.8 0.8 copy_bitcast_fusion.2
  121.7 0.0 copy-done
  121.7 1.4 %copy.18 = f32[27,128,64]{1,2,0:T(8,128)} copy(f32[27,128,64]{2,1,0:T(8,128)S(1)} %copy-done) | data formatting | bytes 1769472
  123.1 0.0 copy-done.2
  123.1 0.9 copy.27
Async XLA Ops:
  0.6 2.2 %copy-start.3 = (bf16[27,64,128]{2,1,0:T(8,128)(2,1)S(1)}, bf16[27,64,128]{2,1,0:T(8,128)(2,1)}, u32[]{:S(2)}) copy-start(bf16[27,64,128]{2,1,0:T(8,128)(2,1)} %param.6) | copy-start | bytes 1327108
  1.9 2.5 %copy-start.4 = (bf16[27,128,64]{1,2,0:T(8,128)(2,1)S(1)}, bf16[27,128,64]{1,2,0:T(8,128)(2,1)}, u32[]{:S(2)}) copy-start(bf16[27,128,64]{1,2,0:T(8,128)(2,1)} %param.5) | copy-start | bytes 1327108
  2.8 2.8 %copy-start.1 = (bf16[1,64,4,8,256]{4,3,2,1,0:T(8,128)(2,1)S(1)}, bf16[1,64,4,8,256]{4,3,2,1,0:T(8,128)(2,1)}, u32[]{:S(2)}) copy-start(bf16[1,64,4,8,256]{4,3,2,1,0:T(8,128)(2,1)} %param.4) | copy-start | bytes 3145732
  119.5 2.1 %copy-start = (f32[27,128,64]{2,1,0:T(8,128)S(1)}, f32[27,128,64]{2,1,0:T(8,128)}, u32[]{:S(2)}) copy-start(f32[27,128,64]{2,1,0:T(8,128)} %get-tuple-element.14) | copy-start | bytes 2654212
  120.8 2.3 %copy-start.2 = (f32[27,64,128]{2,1,0:T(8,128)S(1)}, f32[27,64,128]{2,1,0:T(8,128)}, u32[]{:S(2)}) copy-start(f32[27,64,128]{2,1,0:T(8,128)} %get-tuple-element.19) | copy-start | bytes 2654212

commit v2 on v0

v2 whole, which is shorter than its diff:
```python
import jax
import jax.numpy as jnp
from jax import lax
from jax.experimental import pallas as pl
from jax.experimental.pallas import tpu as pltpu
from jax.sharding import PartitionSpec as P

BF16 = jnp.bfloat16
F32 = jnp.float32
MESH = pl.DeviceIdType.MESH

SIDES = [(dx, dy) for dx in (-1, 0, 1) for dy in (-1, 0, 1) if (dx, dy) != (0, 0)]


def dot(a, b):
    return lax.dot_general(a, b, (((1,), (0,)), ((), ())), preferred_element_type=F32)


def dot_nt(a, b):
    return lax.dot_general(a, b, (((1,), (1,)), ((), ())), preferred_element_type=F32)


def selector(rows, cols, hit):
    row = lax.broadcasted_iota(jnp.int32, (rows, cols), 0)
    col = lax.broadcasted_iota(jnp.int32, (rows, cols), 1)
    return jnp.where(hit(row, col), 1.0, 0.0).astype(BF16)


def sigmoid(u):
    return 0.5 + 0.5 * jnp.tanh(0.5 * u)


def sent_and_landed(side, length):
    if side == 0:
        return (1, length), (1, length)
    if side == 1:
        return (length, 1), (0, 1)
    return (1, 1), (length + 1, 1)


def build_early_weights(ef, w9):
    eye = selector(128, 128, lambda r, c: r == c)
    none = jnp.zeros((64, 128), BF16)

    def body(ae, carry):
        taps = [ef[3 * ae + f] for f in range(3)]
        for p in range(2):
            slots = [none] + taps if p else taps + [none]
            w9[ae, p * 128 : (p + 1) * 128, :] = dot_nt(eye, jnp.concatenate(slots, axis=0)).astype(BF16)
        return carry

    lax.fori_loop(0, 9, body, 0)


def place_taps(block, spread, taps_in, x, first_y, count):
    wide = dot(block, spread[...]).astype(BF16)
    for y in range(count):
        for s in range(4):
            taps_in[x, s * 64 : (s + 1) * 64, pl.ds((first_y + y) * 128, 128)] = wide[
                y * 64 : (y + 1) * 64, s * 128 : (s + 1) * 128
            ]


def early_terms(taps_in, w9, x, Y, shifts):
    total = None
    for a in shifts:
        for e in range(3):
            lanes = pl.ds(pl.multiple_of((2 * Y + e) * 128, 128), 256)
            term = dot(w9[3 * a + e], taps_in[x + a, :, lanes])
            total = term if total is None else total + term
    return total


def early_activation(pre, slopes, x, Y):
    s = sigmoid(pre)
    slopes[x, :, pl.ds(pl.multiple_of(Y * 256, 256), 256)] = s * (1.0 + pre * (1.0 - s))
    act = pre * s
    act = act[:128] + act[128:]
    return act[:, :128] + act[:, 128:]


def early_inner(taps_in, w9, slopes, pool_sum):
    def body(Y, carry):
        own = pl.ds(pl.multiple_of(Y * 256, 256), 256)
        for x, shifts in ((0, (1, 2)), (3, (0, 1))):
            slopes[x, :, own] = early_terms(taps_in, w9, x, Y, shifts)
        for X, x in enumerate((1, 2)):
            pre = early_terms(taps_in, w9, x, Y, (0, 1, 2))
            pool_sum[X, :, pl.ds(pl.multiple_of(Y * 128, 128), 128)] = early_activation(pre, slopes, x, Y)
        return carry

    lax.fori_loop(0, 4, body, 0)


def early_outer(taps_in, w9, slopes, pool_sum, pooled):
    for Y in range(4):
        for X, x, a in ((0, 0, 0), (1, 3, 2)):
            pre = slopes[x, :, Y * 256 : (Y + 1) * 256] + early_terms(taps_in, w9, x, Y, (a,))
            total = pool_sum[X, :, Y * 128 : (Y + 1) * 128] + early_activation(pre, slopes, x, Y)
            pooled[X + 1, 128:256, (Y + 1) * 128 : (Y + 2) * 128] = (total * 0.125).astype(BF16)


def shift_pooled(pooled, xs, first, count):
    shifts = selector(128, 256, lambda r, c: r == jnp.where(c < 128, c - 1, c - 127))
    for x in xs:
        blocks = [pooled[x, 128:256, (first + y) * 128 : (first + y + 1) * 128] for y in range(count)]
        both = dot(jnp.concatenate(blocks, axis=0), shifts).astype(BF16)
        for y in range(count):
            lanes = slice((first + y) * 128, (first + y + 1) * 128)
            rows = slice(y * 128, (y + 1) * 128)
            pooled[x, 0:128, lanes] = both[rows, :128]
            pooled[x, 256:384, lanes] = both[rows, 128:]


def transpose_deep_weights(wd, wdt):
    eye = selector(128, 128, lambda r, c: r == c)

    def body(i, carry):
        for ae in range(3):
            for f in range(3):
                rows = slice(f * 128, (f + 1) * 128)
                wdt[3 * i + ae, rows, :] = dot_nt(eye, wd[9 * i + 3 * ae + f]).astype(BF16)
        return carry

    lax.fori_loop(0, 3, body, 0)


def deep_terms(pooled, wd, X, h, shifts):
    total = None
    for a in shifts:
        for e in range(3):
            weights = jnp.concatenate([wd[9 * a + 3 * e + f] for f in range(3)], axis=1)
            term = dot(weights, pooled[X + a, :, h * 256 + e * 128 : h * 256 + e * 128 + 256])
            total = term if total is None else total + term
    return total


def deep_inner(pooled, wd, pre_deep):
    for h in range(2):
        for X, shifts in ((0, (1, 2)), (1, (0, 1))):
            pre_deep[X, :, h * 256 : (h + 1) * 256] = deep_terms(pooled, wd, X, h, shifts)


def deep_outer(pooled, wd, ct, pre_deep, act, deep_in):
    for X, a in ((0, 0), (1, 2)):
        for h in range(2):
            pre = pre_deep[X, :, h * 256 : (h + 1) * 256] + deep_terms(pooled, wd, X, h, (a,))
            s = sigmoid(pre)
            value = (pre * s).astype(BF16)
            slope = s * (1.0 + pre * (1.0 - s))
            for k in range(2):
                Y, part = 2 * h + k, slice(k * 128, (k + 1) * 128)
                act[Y, X] = value[:, part]
                deep_in[X, :, (Y + 2) * 128 : (Y + 3) * 128] = (ct[Y, X].astype(F32) * slope[:, part]).astype(BF16)


def pooled_terms(deep_in, wdt, pairs, first):
    column = lax.broadcasted_iota(jnp.int32, (128, 128), 1)
    total = None
    for X, a in pairs:
        for e in range(3):
            lanes = slice((first + 2 - e) * 128, (first + 4 - e) * 128)
            term = dot(wdt[3 * a + e], deep_in[X, :, lanes])
            total = term if total is None else total + term
    parts = []
    for k in range(2):
        part = total[:, k * 128 : (k + 1) * 128]
        grad = part[128:256]
        grad += jnp.where(column < 127, pltpu.roll(part[0:128], 127, 1), 0.0)
        grad += jnp.where(column > 0, pltpu.roll(part[256:384], 1, 1), 0.0)
        parts.append(grad)
    return jnp.concatenate(parts, axis=1)


def pooled_outer(deep_in, wdt, send_x):
    for n, pairs in enumerate((((0, 0),), ((1, 2),))):
        for first in (0, 2, 4):
            send_x[n, :, first * 128 : (first + 2) * 128] = pooled_terms(deep_in, wdt, pairs, first).astype(BF16)


def pooled_inner(deep_in, wdt, pooled_grad):
    for X, pairs in enumerate((((0, 1), (1, 0)), ((0, 2), (1, 1)))):
        for first in (0, 2, 4):
            pooled_grad[X, :, first * 128 : (first + 2) * 128] = pooled_terms(deep_in, wdt, pairs, first)


def early_cotangent(pooled_grad, got_x, got_y, got_xy, slopes, early_in):
    for X in range(2):
        grad = pooled_grad[X, :, 128:640] + got_x[X].astype(F32)
        for Y in range(4):
            here = grad[:, Y * 128 : (Y + 1) * 128]
            if Y in (0, 3):
                here += got_y[Y // 3, X].astype(F32) + got_xy[X, Y // 3].astype(F32)
            here *= 0.125
            for x in (2 * X, 2 * X + 1):
                for y in (2 * Y, 2 * Y + 1):
                    lanes = slice(y * 128, (y + 1) * 128)
                    for p in range(2):
                        rows = slice(p * 128, (p + 1) * 128)
                        early_in[x, rows, lanes] = (here * slopes[x, rows, lanes]).astype(BF16)


def deep_gradient(deep_in, pooled, out):
    def body(i, carry):
        a, e = i // 3, i % 3
        lanes = pl.ds(pl.multiple_of(e * 128, 128), 512)
        total = None
        for X in range(2):
            term = dot_nt(deep_in[X, :, 256:768], pooled[X + a, :, lanes])
            total = term if total is None else total + term
        for f in range(3):
            tap = total[:, f * 128 : (f + 1) * 128].astype(BF16).reshape(4, 2, 32, 128)
            for h in range(2):
                out[h, 3 * i + f] = tap[:, h]
        return carry

    lax.fori_loop(0, 9, body, 0)


def early_gradient(early_in, taps_in, out, first, last):
    def body(i, carry):
        a, e = i // 3, i % 3
        lanes = pl.ds(pl.multiple_of(e * 128, 128), 1024)
        total = None
        for x in range(4):
            term = dot_nt(taps_in[x + a, :, lanes], early_in[x])
            total = term if total is None else total + term
        total = (total[:192, :128] + total[64:, 128:]).astype(BF16)
        for f in range(3):
            for h in range(2):
                out[h, 3 * i + f] = total[f * 64 + h * 32 : f * 64 + h * 32 + 32]
        return carry

    lax.fori_loop(first, last, body, 0)


def add_taps(count, out, terms):
    def body(t, carry):
        total = None
        for term in terms:
            value = term(t).astype(F32)
            total = value if total is None else total + value
        out(t, total.astype(BF16))
        return carry

    lax.fori_loop(0, count, body, 0)


def kernel(
    samples, ef, wd_own, ct_own,
    act_out, full,
    sample_ext, taps_in, w9, spread, slopes, pool_sum, pooled, wd, wdt, ct, pre_deep, act, deep_in,
    pooled_grad, send_x, send_y, got_x, got_y, got_xy, early_in,
    dg, dg_pair, dg_sum, dg_chan, eg, eg_pair, part, part_in, eg_chan,
    halo_send, halo_recv, chan_send, chan_recv, pair_send, pair_recv, plane_send, plane_recv,
):
    dp, space, chan = lax.axis_index("dp"), lax.axis_index("space"), lax.axis_index("chan")
    core, column = space % 2, space // 2
    rank = column * 2 + dp

    def side_device(dx, dy):
        return {"dp": dp, "space": (space + dx + 16) % 16, "chan": (chan + dy + 4) % 4}

    def chan_device(j):
        return {"dp": dp, "space": space, "chan": (chan + j) % 4}

    def plane_device(j):
        r = (rank + j) % 16
        return {"dp": r % 2, "space": (r // 2) * 2 + core, "chan": chan}

    sibling = {"dp": dp, "space": column * 2 + 1 - core, "chan": chan}

    barrier = pltpu.get_barrier_semaphore()
    peers = [side_device(dx, dy) for dx, dy in SIDES]
    peers += [chan_device(2), sibling] + [plane_device(j) for j in range(1, 16)]
    for peer in peers:
        pl.semaphore_signal(barrier, inc=1, device_id=peer, device_id_type=MESH)

    build_early_weights(ef, w9)
    spread[...] = selector(256, 512, lambda r, c: r == 2 * (c % 128) + c // 128 - 1)
    part[:, 27:, :, :] = jnp.zeros((2, 5, 32, 128), BF16)
    for X in range(2):
        for lanes in (slice(0, 256), slice(768, 1024)):
            deep_in[X, :, lanes] = jnp.zeros((256, 256), BF16)

    pl.semaphore_wait(barrier, len(peers))

    sends = []

    def describe(src, dst, send_sem, recv_sem, device):
        return pltpu.make_async_remote_copy(
            src_ref=src, dst_ref=dst, send_sem=send_sem, recv_sem=recv_sem, device_id=device, device_id_type=MESH
        )

    def remote(*args):
        copy = describe(*args)
        copy.start()
        sends.append(copy)
        return copy

    def landed(copies):
        for copy in copies:
            copy.wait_recv()

    def over_chan(n, src, dst):
        return [
            remote(src((chan + j) % 4), dst(j), chan_send.at[n, j], chan_recv.at[n, j], chan_device(j)) for j in (1, 2, 3)
        ]

    def pair(n, src, dst):
        return remote(src, dst, pair_send.at[n], pair_recv.at[n], sibling)

    def halo(n, view):
        copies = {}
        for k, (dx, dy) in enumerate(SIDES):
            src, dst = view(dx, dy)
            copies[dx, dy] = remote(src, dst, halo_send.at[n, k], halo_recv.at[n, k], side_device(dx, dy))
        return [copies[0, -1], copies[0, 1]], [copy for (dx, _), copy in copies.items() if dx != 0]

    def sample_view(dx, dy):
        (sx, nx), (tx, _) = sent_and_landed(dx, 4)
        (sy, ny), (ty, _) = sent_and_landed(dy, 8)
        src = samples.at[pl.ds(sx - 1, nx), pl.ds(sy - 1, ny)]
        return src, sample_ext.at[pl.ds(tx, nx), pl.ds(ty, ny)]

    def field_view(ref, first, rows):
        def view(dx, dy):
            (sx, nx), (tx, _) = sent_and_landed(dx, 2)
            (sy, ny), (ty, _) = sent_and_landed(dy, 4)
            block = pl.ds(first, rows)
            src = ref.at[pl.ds(sx, nx), block, pl.ds(sy * 128, ny * 128)]
            return src, ref.at[pl.ds(tx, nx), block, pl.ds(ty * 128, ny * 128)]

        return view

    def clear_y(ref, xs, rows, lanes):
        width = ref.shape[2]
        for at, span in ((0, slice(0, lanes)), (3, slice(width - lanes, width))):

            @pl.when(chan == at)
            def _():
                for x in xs:
                    ref[x, rows, span] = jnp.zeros((rows.stop - rows.start, lanes), BF16)

    def clear_x(ref, rows):
        width = ref.shape[2]
        for at, x in ((0, 0), (15, ref.shape[0] - 1)):

            @pl.when(space == at)
            def _():
                ref[x, rows, :] = jnp.zeros((rows.stop - rows.start, width), BF16)

    sample_y, sample_x = halo(0, sample_view)
    for x in range(4):
        place_taps(samples[x].reshape(512, 256), spread, taps_in, x + 1, 1, 8)
    mine = pl.ds(pl.multiple_of(chan * 64, 64), 64)
    wd[:, mine, :] = wd_own[...]
    ct[:, :, mine, :] = ct_own[pl.ds(pl.multiple_of(chan * 4, 4), 4)]
    landed(sample_y)

    half = pl.ds(pl.multiple_of(core * 32, 32), 32)

    def half_of(c):
        return wd.at[:, pl.ds(pl.multiple_of(c * 64 + core * 32, 32), 32), :]

    wd_copies = over_chan(0, lambda c: wd_own.at[:, half, :], lambda j: half_of(chan))
    for y in (0, 9):
        for x in range(1, 5):
            place_taps(sample_ext[x, y], spread, taps_in, x, y, 1)
    clear_y(taps_in, range(1, 5), slice(0, 256), 128)
    early_inner(taps_in, w9, slopes, pool_sum)
    ct_copies = over_chan(
        1, lambda c: ct_own.at[pl.ds(pl.multiple_of(c * 4, 4), 4)], lambda j: ct.at[:, :, mine, :]
    )
    landed(sample_x)
    for x in (0, 5):
        place_taps(sample_ext[x].reshape(640, 256), spread, taps_in, x, 0, 10)
    clear_y(taps_in, (0, 5), slice(0, 256), 128)
    clear_x(taps_in, slice(0, 256))
    early_outer(taps_in, w9, slopes, pool_sum, pooled)

    pooled_y, pooled_x = halo(1, field_view(pooled, 128, 128))
    shift_pooled(pooled, (1, 2), 1, 4)
    wd_halves = []
    for j, copy in zip((1, 2, 3), wd_copies):
        landed([copy])
        block = half_of((chan - j + 4) % 4)
        wd_halves.append(remote(block, block, chan_send.at[2, j], chan_recv.at[2, j], sibling))
    landed(pooled_y)
    clear_y(pooled, (1, 2), slice(128, 256), 128)
    shift_pooled(pooled, (1, 2), 0, 1)
    shift_pooled(pooled, (1, 2), 5, 1)
    for j in (1, 2, 3):
        theirs = pl.ds(pl.multiple_of((chan - j + 4) % 4 * 64 + (1 - core) * 32, 32), 32)
        block = wd.at[:, theirs, :]
        describe(block, block, chan_send.at[2, j], chan_recv.at[2, j], sibling).wait_recv()
    deep_inner(pooled, wd, pre_deep)
    landed(pooled_x)
    clear_y(pooled, (0, 3), slice(128, 256), 128)
    clear_x(pooled, slice(128, 256))
    shift_pooled(pooled, (0, 3), 0, 6)
    transpose_deep_weights(wd, wdt)
    landed(ct_copies)
    deep_outer(pooled, wd, ct, pre_deep, act, deep_in)

    pooled_outer(deep_in, wdt, send_x)
    grad_copies = []
    for n, dx in enumerate((-1, 1)):
        for dy in (-1, 0, 1):
            at, count = {-1: (0, 1), 0: (1, 4), 1: (5, 1)}[dy]
            src = send_x.at[n, :, pl.ds(at * 128, count * 128)]
            dst = got_x.at[1 - n] if dy == 0 else got_xy.at[1 - n, 0 if dy > 0 else 1]
            k = SIDES.index((dx, dy))
            grad_copies.append(remote(src, dst, halo_send.at[2, k], halo_recv.at[2, k], side_device(dx, dy)))
    pooled_inner(deep_in, wdt, pooled_grad)
    for n, (dy, at) in enumerate(((-1, 0), (1, 5))):
        for X in range(2):
            send_y[n, X] = pooled_grad[X, :, at * 128 : (at + 1) * 128].astype(BF16)
        k = SIDES.index((0, dy))
        grad_copies.append(
            remote(send_y.at[n], got_y.at[1 - n], halo_send.at[2, k], halo_recv.at[2, k], side_device(0, dy))
        )

    deep_gradient(deep_in, pooled, dg)
    dg_pair_copy = pair(0, dg.at[1 - core], dg_pair)
    landed(grad_copies)
    for at, n in ((0, 0), (15, 1)):

        @pl.when(space == at)
        def _():
            got_x[n] = jnp.zeros((128, 512), BF16)
            got_xy[n] = jnp.zeros((2, 128, 128), BF16)

    for at, n in ((0, 0), (3, 1)):

        @pl.when(chan == at)
        def _():
            got_y[n] = jnp.zeros((2, 128, 128), BF16)
            for m in range(2):
                got_xy[m, n] = jnp.zeros((128, 128), BF16)

    early_cotangent(pooled_grad, got_x, got_y, got_xy, slopes, early_in)
    early_gradient(early_in, taps_in, eg, 0, 2)
    landed([dg_pair_copy])

    def put_sum(t, value):
        dg_sum[:, t] = value

    add_taps(27, put_sum, [lambda t: dg[core, t], lambda t: dg_pair[t]])
    dg_copies = over_chan(3, lambda c: dg_sum.at[c], lambda j: dg_chan.at[j])
    early_gradient(early_in, taps_in, eg, 2, 9)
    eg_pair_copy = pair(1, eg.at[1 - core], eg_pair)

    def put_part(n):
        def put(t, value):
            part[n, t] = value

        return put

    def taps_of(r):
        return pl.ds(r * 2, 2)

    own = taps_of(rank)

    def plane_scatter(n):
        copies = []
        for j in range(1, 16):
            src = part.at[n, taps_of((rank + j) % 16)]
            copies.append(remote(src, part_in.at[n, j], plane_send.at[n, j], plane_recv.at[n, j], plane_device(j)))
        return copies

    def plane_sum(n):
        summed = part[n, own].astype(F32)
        for j in range(1, 16):
            summed += part_in[n, j].astype(F32)
        return summed

    def plane_gather(n):
        block = full.at[n, own, half, :]
        for j in range(1, 16):
            remote(block, block, plane_send.at[2 + n, j], plane_recv.at[2 + n, j], plane_device(j))

    def plane_gathered(n):
        for j in range(1, 16):
            theirs = full.at[n, taps_of((rank - j + 16) % 16), half, :]
            describe(theirs, theirs, plane_send.at[2 + n, j], plane_recv.at[2 + n, j], plane_device(j)).wait_recv()

    def halves(n):
        block = full.at[n, pl.ds(0, 27), half, :]
        pair(2 + n, block, block)

    def halves_landed(n):
        block = full.at[n, pl.ds(0, 27), pl.ds(pl.multiple_of(32 - core * 32, 32), 32), :]
        describe(block, block, pair_send.at[2 + n], pair_recv.at[2 + n], sibling).wait_recv()

    landed([eg_pair_copy])
    add_taps(27, put_part(1), [lambda t: eg[core, t], lambda t: eg_pair[t]])
    eg_copies = plane_scatter(1)
    landed(dg_copies)
    add_taps(27, put_part(0), [lambda t: dg_sum[chan, t]] + [lambda t, j=j: dg_chan[j, t] for j in (1, 2, 3)])
    dg_plane = plane_scatter(0)
    here = pl.ds(pl.multiple_of(chan * 4, 4), 4)
    act_copies = over_chan(
        4, lambda c: act.at[:, :, pl.ds(pl.multiple_of(c * 64, 64), 64), :], lambda j: act_out.at[here]
    )
    act_out[here] = act[:, :, mine, :]
    landed(eg_copies)
    eg_chan[chan] = plane_sum(1)
    over_chan(5, lambda c: eg_chan.at[chan], lambda j: eg_chan.at[chan])
    landed(dg_plane)
    full[0, own, half, :] = plane_sum(0).astype(BF16)
    plane_gather(0)
    for j in (1, 2, 3):
        block = eg_chan.at[(chan - j + 4) % 4]
        describe(block, block, chan_send.at[5, j], chan_recv.at[5, j], chan_device(j)).wait_recv()
    full[1, own, half, :] = ((eg_chan[0] + eg_chan[1]) + (eg_chan[2] + eg_chan[3])).astype(BF16)
    plane_gather(1)
    plane_gathered(0)
    halves(0)
    plane_gathered(1)
    halves(1)
    halves_landed(0)
    halves_landed(1)

    landed(act_copies)
    for copy in sends:
        copy.wait_send()


def on_device(samples, early_filters, deep_filters, deep_cotangent):
    samples = samples[0].transpose(1, 2, 0, 3)
    early_filters = early_filters.transpose(0, 2, 1)
    deep_cotangent = deep_cotangent[0].transpose(2, 1, 0, 3)
    act, grads = pl.pallas_call(
        kernel,
        out_shape=(
            jax.ShapeDtypeStruct((16, 2, 64, 128), BF16),
            jax.ShapeDtypeStruct((2, 32, 64, 128), BF16),
        ),
        in_specs=[pl.BlockSpec(memory_space=pltpu.VMEM)] * 4,
        out_specs=[pl.BlockSpec(memory_space=pltpu.VMEM)] * 2,
        scratch_shapes=[
            pltpu.VMEM((6, 10, 64, 256), BF16),
            pltpu.VMEM((6, 256, 1280), BF16),
            pltpu.VMEM((9, 256, 256), BF16),
            pltpu.VMEM((256, 512), BF16),
            pltpu.VMEM((4, 256, 1024), F32),
            pltpu.VMEM((2, 128, 512), F32),
            pltpu.VMEM((4, 384, 768), BF16),
            pltpu.VMEM((27, 256, 128), BF16),
            pltpu.VMEM((9, 384, 256), BF16),
            pltpu.VMEM((4, 2, 256, 128), BF16),
            pltpu.VMEM((2, 256, 512), F32),
            pltpu.VMEM((4, 2, 256, 128), BF16),
            pltpu.VMEM((2, 256, 1024), BF16),
            pltpu.VMEM((2, 128, 768), F32),
            pltpu.VMEM((2, 128, 768), BF16),
            pltpu.VMEM((2, 2, 128, 128), BF16),
            pltpu.VMEM((2, 128, 512), BF16),
            pltpu.VMEM((2, 2, 128, 128), BF16),
            pltpu.VMEM((2, 2, 128, 128), BF16),
            pltpu.VMEM((4, 256, 1024), BF16),
            pltpu.VMEM((2, 27, 4, 32, 128), BF16),
            pltpu.VMEM((27, 4, 32, 128), BF16),
            pltpu.VMEM((4, 27, 32, 128), BF16),
            pltpu.VMEM((4, 27, 32, 128), BF16),
            pltpu.VMEM((2, 27, 32, 128), BF16),
            pltpu.VMEM((27, 32, 128), BF16),
            pltpu.VMEM((2, 32, 32, 128), BF16),
            pltpu.VMEM((2, 16, 2, 32, 128), BF16),
            pltpu.VMEM((4, 2, 32, 128), F32),
            pltpu.SemaphoreType.DMA((3, 8)),
            pltpu.SemaphoreType.DMA((3, 8)),
            pltpu.SemaphoreType.DMA((6, 4)),
            pltpu.SemaphoreType.DMA((6, 4)),
            pltpu.SemaphoreType.DMA((4,)),
            pltpu.SemaphoreType.DMA((4,)),
            pltpu.SemaphoreType.DMA((4, 16)),
            pltpu.SemaphoreType.DMA((4, 16)),
        ],
        compiler_params=pltpu.CompilerParams(
            collective_id=0, has_side_effects=True, vmem_limit_bytes=56 * 1024 * 1024
        ),
        name="conv_step",
    )(samples, early_filters, deep_filters, deep_cotangent)
    grads = grads[:, :27].astype(F32)
    return act.transpose(2, 1, 0, 3)[None], grads[0], grads[1].transpose(0, 2, 1)


def solution(mesh):
    placed = (
        P("dp", None, "space", "chan", None),
        P(),
        P(None, "chan", None),
        P("dp", "chan", "space", None, None),
    )
    return jax.shard_map(
        on_device,
        mesh=mesh,
        in_specs=placed,
        out_specs=(P("dp", "chan", "space", None, None), P(None, "chan", None), P()),
        check_vma=False,
    )
```

time: 643 us -> 93.3 us (0.15)
  waiting for transfers between devices: 295 us -> 0 us
  matrix products: 265 us -> 0 us
  Pallas kernels: 0 us -> 83.8 us
  starting transfers between devices: 28.8 us -> 0 us
  other arithmetic: 18.7 us -> 1.36 us
  between operations: 15.3 us -> 0.66 us
  local copies, waits for them, and re-layouts: 15.4 us -> 7.27 us
    dot_general x135 -> x0, matrix products: 265 us -> none  [the longest x54 129 us: forward_conv(): jnp.einsum('oc,scxyz->soxyz', filters[tap_index], tap_slice(padded, tap_o...]
    psum x2 -> x0, waiting for transfers between devices: 222 us -> none  [the longest x1 152 us: on_device(): lax.psum(filter_grad(early_in, bordered, extent_early), ('dp', 'space', '...]
    pallas_call x0 -> x1, Pallas kernels: none -> 83.8 us  [on_device(): pl.pallas_call(kernel, out_shape=(jax.ShapeDtypeStruct((16, 2, 64, 128),...]
    unnamed x5 -> x0, waiting for transfers between devices: 36.9 us -> none
    ppermute x8 -> x0, starting transfers between devices: 28.6 us -> none  [the longest x4 21.6 us: with_halo(): before = lax.ppermute(last, axis, up)]
    all_gather x1 -> x0, waiting for transfers between devices: 25.1 us -> none  [on_device(): slab = lax.all_gather(pooled, 'chan', axis=3, tiled=True)]
    ppermute x8 -> x0, waiting for transfers between devices: 11.2 us -> none  [the longest x4 7.31 us: with_halo(): before = lax.ppermute(last, axis, up)]
    concatenate x3 -> x0, other arithmetic: 9.44 us -> none  [with_halo(): value = jnp.concatenate([before, value, after], axis=dim)]
  transfers between devices with their start and end apart: 12 -> 0, of which waited for: 7 -> 0; matrix products, arithmetic and copies ran while one was open for 13% -> 0% of each run, Pallas kernels for 0% -> 0%
where the time goes in v2:
time: 93.3 us; the launch traced here: 93.1 us
  Pallas kernels  83.8 us (90%)
  local copies, waits for them, and re-layouts  7.27 us (8%)
  other arithmetic  1.36 us (1%)
    pallas_call x1, Pallas kernels, on_device(): pl.pallas_call(kernel, out_shape=(jax.ShapeDtypeStruct((16, 2, 64, 128),...  83.8 us
    unnamed x5, local copies, waits for them, and re-layouts  5.86 us

profile of v2, /device:TPU:1, one launch (start us, length us, event | category | flops | bytes accessed | tf_op | source)
XLA Modules:
  0.0 93.1 jit_solution(11817018817142690302)
XLA Ops:
  0.6 0.0 copy-start
  0.6 2.1 %copy.13 = bf16[1,64,2,16,128]{4,1,2,3,0:T(8,128)(2,1)} copy(bf16[1,64,2,16,128]{4,3,2,1,0:T(8,128)(2,1)} %param.7) | data formatting | bytes 1048576 | tf_op args[3]
  2.8 0.0 copy-done
  2.8 1.6 %copy.12 = bf16[1,64,4,8,256]{4,1,3,2,0:T(8,128)(2,1)} copy(bf16[1,64,4,8,256]{4,3,2,1,0:T(8,128)(2,1)S(1)} %copy-done) | data formatting | bytes 2097152 | tf_op args[0]
  4.3 83.8 %conv_step.1 = (bf16[16,2,64,128]{3,2,1,0:T(8,128)(2,1)}, bf16[2,32,64,128]{3,2,1,0:T(8,128)(2,1)}) custom-call(bf16[4,8,64,256]{3,2,1,0:T(8,128)(2,1)} %bitcast.20, bf16[27,64,128]{2,1,0:T(8,128)(2,1)} %bitcast.23, bf16[27,64,128]{2,1,0:T(8,128)(2,1)} %wd_own.1, bf16[16,2,64,128]{3,2,1,0:T(8,128)(2,1)} %bitcast.21), custom_call_target="tpu_custom_call" | custom-call | tf_op jit(solution)/shard_map/conv_step/pallas_call | solution.py:534
  88.1 2.2 %copy.9 = bf16[1,64,2,16,128]{4,3,2,1,0:T(8,128)(2,1)} copy(bf16[1,64,2,16,128]{4,1,2,3,0:T(8,128)(2,1)} %bitcast.22) | data formatting | bytes 1048576
  90.3 1.4 %slice_convert_fusion = f32[2,27,64,128]{3,2,1,0:T(8,128)S(1)} fusion(bf16[2,32,64,128]{3,2,1,0:T(8,128)(2,1)} %get-tuple-element.6), kind=kLoop, calls=%fused_computation.3 | loop fusion | flops 442368 | bytes 2654208 | tf_op jit(solution)/shard_map/convert_element_type | solution.py:586
  91.6 1.4 %slice_bitcast_fusion = (f32[27,128,64]{1,2,0:T(8,128)}, f32[27,64,128]{2,1,0:T(8,128)}) fusion(f32[2,27,64,128]{3,2,1,0:T(8,128)S(1)} %slice_convert_fusion), kind=kLoop, calls=%fused_computation.1 | loop fusion | bytes 3538944 | tf_op jit(solution)/shard_map/transpose | solution.py:587
Async XLA Ops:
  0.6 2.1 %copy-start = (bf16[1,64,4,8,256]{4,3,2,1,0:T(8,128)(2,1)S(1)}, bf16[1,64,4,8,256]{4,3,2,1,0:T(8,128)(2,1)}, u32[]{:S(2)}) copy-start(bf16[1,64,4,8,256]{4,3,2,1,0:T(8,128)(2,1)} %param.4) | copy-start | bytes 3145732

commit v3 on v2

--- a/solution.py
+++ b/solution.py
@@ -42,14 +42,55 @@
     eye = selector(128, 128, lambda r, c: r == c)
     none = jnp.zeros((64, 128), BF16)
 
-    def body(ae, carry):
-        taps = [ef[3 * ae + f] for f in range(3)]
-        for p in range(2):
-            slots = [none] + taps if p else taps + [none]
-            w9[ae, p * 128 : (p + 1) * 128, :] = dot_nt(eye, jnp.concatenate(slots, axis=0)).astype(BF16)
+    def body(i, carry):
+        for ae in range(3):
+            taps = [ef[9 * i + 3 * ae + f] for f in range(3)]
+            for p in range(2):
+                slots = [none] + taps if p else taps + [none]
+                rows = slice(p * 128, (p + 1) * 128)
+                w9[3 * i + ae, rows, :] = dot_nt(eye, jnp.concatenate(slots, axis=0)).astype(BF16)
         return carry
 
-    lax.fori_loop(0, 9, body, 0)
+    lax.fori_loop(0, 3, body, 0)
+
+
+def cells_first(samples_raw, samples):
+    swap = selector(256, 256, lambda r, c: c == (r % 32) * 8 + r // 32)
+
+    def body(x, carry):
+        for n in range(2):
+            block = samples_raw[n * 32 : (n + 1) * 32, x].astype(F32).reshape(256, 256).astype(BF16)
+            block = dot(swap, block).astype(BF16)
+            for y in range(8):
+                samples[x, y, n * 32 : (n + 1) * 32, :] = block[y * 32 : (y + 1) * 32]
+        return carry
+
+    lax.fori_loop(0, 4, body, 0)
+
+
+def row_swap():
+    return selector(256, 256, lambda r, c: c == (r % 16) * 16 + r // 16)
+
+
+def deep_cells_first(raw, out):
+    swap = row_swap()
+    for n in range(4):
+        rows = slice(n * 16, (n + 1) * 16)
+        block = jnp.concatenate([raw[rows, X].reshape(256, 128) for X in range(2)], axis=1)
+        block = dot(swap, block).astype(BF16)
+        for Y in range(16):
+            for X in range(2):
+                out[Y, X, rows, :] = block[Y * 16 : (Y + 1) * 16, X * 128 : (X + 1) * 128]
+
+
+def deep_channels_first(raw, out):
+    swap = row_swap()
+    for n in range(4):
+        rows = slice(n * 16, (n + 1) * 16)
+        block = [jnp.concatenate([raw[Y, X, rows, :] for Y in range(16)], axis=0) for X in range(2)]
+        block = dot(swap, jnp.concatenate(block, axis=1)).astype(BF16)
+        for X in range(2):
+            out[rows, X] = block[:, X * 128 : (X + 1) * 128].reshape(16, 16, 128)
 
 
 def place_taps(block, spread, taps_in, x, first_y, count):
@@ -79,7 +120,7 @@
     return act[:, :128] + act[:, 128:]
 
 
-def early_inner(taps_in, w9, slopes, pool_sum):
+def early_inner(taps_in, w9, slopes, pool_sum, first, last):
     def body(Y, carry):
         own = pl.ds(pl.multiple_of(Y * 256, 256), 256)
         for x, shifts in ((0, (1, 2)), (3, (0, 1))):
@@ -89,7 +130,7 @@
             pool_sum[X, :, pl.ds(pl.multiple_of(Y * 128, 128), 128)] = early_activation(pre, slopes, x, Y)
         return carry
 
-    lax.fori_loop(0, 4, body, 0)
+    lax.fori_loop(first, last, body, 0)
 
 
 def early_outer(taps_in, w9, slopes, pool_sum, pooled):
@@ -178,9 +219,9 @@
             send_x[n, :, first * 128 : (first + 2) * 128] = pooled_terms(deep_in, wdt, pairs, first).astype(BF16)
 
 
-def pooled_inner(deep_in, wdt, pooled_grad):
+def pooled_inner(deep_in, wdt, pooled_grad, firsts):
     for X, pairs in enumerate((((0, 1), (1, 0)), ((0, 2), (1, 1)))):
-        for first in (0, 2, 4):
+        for first in firsts:
             pooled_grad[X, :, first * 128 : (first + 2) * 128] = pooled_terms(deep_in, wdt, pairs, first)
 
 
@@ -217,7 +258,7 @@
     lax.fori_loop(0, 9, body, 0)
 
 
-def early_gradient(early_in, taps_in, out, first, last):
+def early_gradient(early_in, taps_in, out):
     def body(i, carry):
         a, e = i // 3, i % 3
         lanes = pl.ds(pl.multiple_of(e * 128, 128), 1024)
@@ -231,7 +272,7 @@
                 out[h, 3 * i + f] = total[f * 64 + h * 32 : f * 64 + h * 32 + 32]
         return carry
 
-    lax.fori_loop(first, last, body, 0)
+    lax.fori_loop(0, 9, body, 0)
 
 
 def add_taps(count, out, terms):
@@ -247,12 +288,12 @@
 
 
 def kernel(
-    samples, ef, wd_own, ct_own,
-    act_out, full,
-    sample_ext, taps_in, w9, spread, slopes, pool_sum, pooled, wd, wdt, ct, pre_deep, act, deep_in,
+    samples_raw, ef, wd_own, ct_raw,
+    act_out, dg_out, eg_out,
+    samples, ct_own, act_in, full, sample_ext, taps_in, w9, spread, slopes, pool_sum, pooled, wd, wdt, ct, pre_deep, act, deep_in,
     pooled_grad, send_x, send_y, got_x, got_y, got_xy, early_in,
     dg, dg_pair, dg_sum, dg_chan, eg, eg_pair, part, part_in, eg_chan,
-    halo_send, halo_recv, chan_send, chan_recv, pair_send, pair_recv, plane_send, plane_recv,
+    halo_send, halo_recv, x_send, x_recv, chan_send, chan_recv, pair_send, pair_recv, plane_send, plane_recv,
 ):
     dp, space, chan = lax.axis_index("dp"), lax.axis_index("space"), lax.axis_index("chan")
     core, column = space % 2, space // 2
@@ -263,6 +304,9 @@
 
     def chan_device(j):
         return {"dp": dp, "space": space, "chan": (chan + j) % 4}
+
+    def x_device(j):
+        return {"dp": dp, "space": (space + 4 * j) % 16, "chan": chan}
 
     def plane_device(j):
         r = (rank + j) % 16
@@ -276,13 +320,9 @@
     for peer in peers:
         pl.semaphore_signal(barrier, inc=1, device_id=peer, device_id_type=MESH)
 
+    cells_first(samples_raw, samples)
     build_early_weights(ef, w9)
     spread[...] = selector(256, 512, lambda r, c: r == 2 * (c % 128) + c // 128 - 1)
-    part[:, 27:, :, :] = jnp.zeros((2, 5, 32, 128), BF16)
-    for X in range(2):
-        for lanes in (slice(0, 256), slice(768, 1024)):
-            deep_in[X, :, lanes] = jnp.zeros((256, 256), BF16)
-
     pl.semaphore_wait(barrier, len(peers))
 
     sends = []
@@ -351,27 +391,40 @@
                 ref[x, rows, :] = jnp.zeros((rows.stop - rows.start, width), BF16)
 
     sample_y, sample_x = halo(0, sample_view)
+    mine = pl.ds(pl.multiple_of(chan * 64, 64), 64)
+    half = pl.ds(pl.multiple_of(core * 32, 32), 32)
+    wd[0:27, mine, :] = wd_own[...]
+    wd[27, mine, :] = jnp.zeros((64, 128), BF16)
     for x in range(4):
         place_taps(samples[x].reshape(512, 256), spread, taps_in, x + 1, 1, 8)
-    mine = pl.ds(pl.multiple_of(chan * 64, 64), 64)
-    wd[:, mine, :] = wd_own[...]
+    deep_cells_first(ct_raw, ct_own)
     ct[:, :, mine, :] = ct_own[pl.ds(pl.multiple_of(chan * 4, 4), 4)]
+    part[:, 27:, :, :] = jnp.zeros((2, 5, 32, 128), BF16)
+    for X in range(2):
+        for lanes in (slice(0, 256), slice(768, 1024)):
+            deep_in[X, :, lanes] = jnp.zeros((256, 256), BF16)
+
     landed(sample_y)
 
-    half = pl.ds(pl.multiple_of(core * 32, 32), 32)
-
-    def half_of(c):
-        return wd.at[:, pl.ds(pl.multiple_of(c * 64 + core * 32, 32), 32), :]
-
-    wd_copies = over_chan(0, lambda c: wd_own.at[:, half, :], lambda j: half_of(chan))
+    def some_of(c, taps, of_core):
+        return wd.at[taps, pl.ds(pl.multiple_of(c * 64 + of_core * 32, 32), 32), :]
+
+    my_taps = pl.ds(space // 4 * 7, 7)
+    wd_copies = over_chan(0, lambda c: some_of(chan, my_taps, core), lambda j: some_of(chan, my_taps, core))
+    ct_copies = over_chan(
+        1, lambda c: ct_own.at[pl.ds(pl.multiple_of(c * 4, 4), 4)], lambda j: ct.at[:, :, mine, :]
+    )
     for y in (0, 9):
         for x in range(1, 5):
             place_taps(sample_ext[x, y], spread, taps_in, x, y, 1)
     clear_y(taps_in, range(1, 5), slice(0, 256), 128)
-    early_inner(taps_in, w9, slopes, pool_sum)
-    ct_copies = over_chan(
-        1, lambda c: ct_own.at[pl.ds(pl.multiple_of(c * 4, 4), 4)], lambda j: ct.at[:, :, mine, :]
-    )
+    early_inner(taps_in, w9, slopes, pool_sum, 0, 1)
+    for j, copy in zip((1, 2, 3), wd_copies):
+        landed([copy])
+        block = some_of((chan - j + 4) % 4, my_taps, core)
+        for i in (1, 2, 3):
+            remote(block, block, x_send.at[j, i], x_recv.at[j, i], x_device(i))
+    early_inner(taps_in, w9, slopes, pool_sum, 1, 4)
     landed(sample_x)
     for x in (0, 5):
         place_taps(sample_ext[x].reshape(640, 256), spread, taps_in, x, 0, 10)
@@ -381,25 +434,25 @@
 
     pooled_y, pooled_x = halo(1, field_view(pooled, 128, 128))
     shift_pooled(pooled, (1, 2), 1, 4)
-    wd_halves = []
-    for j, copy in zip((1, 2, 3), wd_copies):
-        landed([copy])
-        block = half_of((chan - j + 4) % 4)
-        wd_halves.append(remote(block, block, chan_send.at[2, j], chan_recv.at[2, j], sibling))
+    for j in (1, 2, 3):
+        for i in (1, 2, 3):
+            block = some_of((chan - j + 4) % 4, pl.ds((space // 4 - i + 4) % 4 * 7, 7), core)
+            describe(block, block, x_send.at[j, i], x_recv.at[j, i], x_device(i)).wait_recv()
+        block = some_of((chan - j + 4) % 4, pl.ds(0, 27), core)
+        remote(block, block, chan_send.at[2, j], chan_recv.at[2, j], sibling)
     landed(pooled_y)
     clear_y(pooled, (1, 2), slice(128, 256), 128)
     shift_pooled(pooled, (1, 2), 0, 1)
     shift_pooled(pooled, (1, 2), 5, 1)
     for j in (1, 2, 3):
-        theirs = pl.ds(pl.multiple_of((chan - j + 4) % 4 * 64 + (1 - core) * 32, 32), 32)
-        block = wd.at[:, theirs, :]
+        block = some_of((chan - j + 4) % 4, pl.ds(0, 27), 1 - core)
         describe(block, block, chan_send.at[2, j], chan_recv.at[2, j], sibling).wait_recv()
     deep_inner(pooled, wd, pre_deep)
+    transpose_deep_weights(wd, wdt)
     landed(pooled_x)
     clear_y(pooled, (0, 3), slice(128, 256), 128)
     clear_x(pooled, slice(128, 256))
     shift_pooled(pooled, (0, 3), 0, 6)
-    transpose_deep_weights(wd, wdt)
     landed(ct_copies)
     deep_outer(pooled, wd, ct, pre_deep, act, deep_in)
 
@@ -412,7 +465,7 @@
             dst = got_x.at[1 - n] if dy == 0 else got_xy.at[1 - n, 0 if dy > 0 else 1]
             k = SIDES.index((dx, dy))
             grad_copies.append(remote(src, dst, halo_send.at[2, k], halo_recv.at[2, k], side_device(dx, dy)))
-    pooled_inner(deep_in, wdt, pooled_grad)
+    pooled_inner(deep_in, wdt, pooled_grad, (0, 4))
     for n, (dy, at) in enumerate(((-1, 0), (1, 5))):
         for X in range(2):
             send_y[n, X] = pooled_grad[X, :, at * 128 : (at + 1) * 128].astype(BF16)
@@ -423,6 +476,14 @@
 
     deep_gradient(deep_in, pooled, dg)
     dg_pair_copy = pair(0, dg.at[1 - core], dg_pair)
+    pooled_inner(deep_in, wdt, pooled_grad, (2,))
+
+    def put_sum(t, value):
+        dg_sum[:, t] = value
+
+    landed([dg_pair_copy])
+    add_taps(27, put_sum, [lambda t: dg[core, t], lambda t: dg_pair[t]])
+    dg_copies = over_chan(3, lambda c: dg_sum.at[c], lambda j: dg_chan.at[j])
     landed(grad_copies)
     for at, n in ((0, 0), (15, 1)):
 
@@ -440,15 +501,7 @@
                 got_xy[m, n] = jnp.zeros((128, 128), BF16)
 
     early_cotangent(pooled_grad, got_x, got_y, got_xy, slopes, early_in)
-    early_gradient(early_in, taps_in, eg, 0, 2)
-    landed([dg_pair_copy])
-
-    def put_sum(t, value):
-        dg_sum[:, t] = value
-
-    add_taps(27, put_sum, [lambda t: dg[core, t], lambda t: dg_pair[t]])
-    dg_copies = over_chan(3, lambda c: dg_sum.at[c], lambda j: dg_chan.at[j])
-    early_gradient(early_in, taps_in, eg, 2, 9)
+    early_gradient(early_in, taps_in, eg)
     eg_pair_copy = pair(1, eg.at[1 - core], eg_pair)
 
     def put_part(n):
@@ -501,9 +554,9 @@
     dg_plane = plane_scatter(0)
     here = pl.ds(pl.multiple_of(chan * 4, 4), 4)
     act_copies = over_chan(
-        4, lambda c: act.at[:, :, pl.ds(pl.multiple_of(c * 64, 64), 64), :], lambda j: act_out.at[here]
+        4, lambda c: act.at[:, :, pl.ds(pl.multiple_of(c * 64, 64), 64), :], lambda j: act_in.at[here]
     )
-    act_out[here] = act[:, :, mine, :]
+    act_in[here] = act[:, :, mine, :]
     landed(eg_copies)
     eg_chan[chan] = plane_sum(1)
     over_chan(5, lambda c: eg_chan.at[chan], lambda j: eg_chan.at[chan])
@@ -517,29 +570,36 @@
     plane_gather(1)
     plane_gathered(0)
     halves(0)
+    landed(act_copies)
+    deep_channels_first(act_in, act_out)
     plane_gathered(1)
     halves(1)
     halves_landed(0)
+    for t in range(27):
+        dg_out[t] = full[0, t].astype(F32)
     halves_landed(1)
-
-    landed(act_copies)
+    for t in range(27):
+        eg_out[t] = full[1, t].astype(F32)
+
     for copy in sends:
         copy.wait_send()
 
 
 def on_device(samples, early_filters, deep_filters, deep_cotangent):
-    samples = samples[0].transpose(1, 2, 0, 3)
-    early_filters = early_filters.transpose(0, 2, 1)
-    deep_cotangent = deep_cotangent[0].transpose(2, 1, 0, 3)
-    act, grads = pl.pallas_call(
+    act, deep_grad, early_grad = pl.pallas_call(
         kernel,
         out_shape=(
-            jax.ShapeDtypeStruct((16, 2, 64, 128), BF16),
-            jax.ShapeDtypeStruct((2, 32, 64, 128), BF16),
+            jax.ShapeDtypeStruct((64, 2, 16, 128), BF16),
+            jax.ShapeDtypeStruct((27, 64, 128), F32),
+            jax.ShapeDtypeStruct((27, 64, 128), F32),
         ),
         in_specs=[pl.BlockSpec(memory_space=pltpu.VMEM)] * 4,
-        out_specs=[pl.BlockSpec(memory_space=pltpu.VMEM)] * 2,
+        out_specs=[pl.BlockSpec(memory_space=pltpu.VMEM)] * 3,
         scratch_shapes=[
+            pltpu.VMEM((4, 8, 64, 256), BF16),
+            pltpu.VMEM((16, 2, 64, 128), BF16),
+            pltpu.VMEM((16, 2, 64, 128), BF16),
+            pltpu.VMEM((2, 32, 64, 128), BF16),
             pltpu.VMEM((6, 10, 64, 256), BF16),
             pltpu.VMEM((6, 256, 1280), BF16),
             pltpu.VMEM((9, 256, 256), BF16),
@@ -547,7 +607,7 @@
             pltpu.VMEM((4, 256, 1024), F32),
             pltpu.VMEM((2, 128, 512), F32),
             pltpu.VMEM((4, 384, 768), BF16),
-            pltpu.VMEM((27, 256, 128), BF16),
+            pltpu.VMEM((28, 256, 128), BF16),
             pltpu.VMEM((9, 384, 256), BF16),
             pltpu.VMEM((4, 2, 256, 128), BF16),
             pltpu.VMEM((2, 256, 512), F32),
@@ -571,6 +631,8 @@
             pltpu.VMEM((4, 2, 32, 128), F32),
             pltpu.SemaphoreType.DMA((3, 8)),
             pltpu.SemaphoreType.DMA((3, 8)),
+            pltpu.SemaphoreType.DMA((4, 4)),
+            pltpu.SemaphoreType.DMA((4, 4)),
             pltpu.SemaphoreType.DMA((6, 4)),
             pltpu.SemaphoreType.DMA((6, 4)),
             pltpu.SemaphoreType.DMA((4,)),
@@ -582,9 +644,8 @@
             collective_id=0, has_side_effects=True, vmem_limit_bytes=56 * 1024 * 1024
         ),
         name="conv_step",
-    )(samples, early_filters, deep_filters, deep_cotangent)
-    grads = grads[:, :27].astype(F32)
-    return act.transpose(2, 1, 0, 3)[None], grads[0], grads[1].transpose(0, 2, 1)
+    )(samples[0], early_filters.transpose(0, 2, 1), deep_filters, deep_cotangent[0])
+    return act[None], deep_grad, early_grad.transpose(0, 2, 1)
 
 
 def solution(mesh):

time: 93.3 us -> 84.8 us (0.909)
  Pallas kernels: 83.8 us -> 79.6 us
  local copies, waits for them, and re-layouts: 7.27 us -> 4.35 us
  other arithmetic: 1.36 us -> 0 us
    pallas_call x1, Pallas kernels: 83.8 us -> 79.6 us  [on_device(): pl.pallas_call(kernel, out_shape=(jax.ShapeDtypeStruct((64, 2, 16, 128),...]
    unnamed x5 -> x7, local copies, waits for them, and re-layouts: 5.86 us -> 4.35 us
    transpose x1 -> x0, local copies, waits for them, and re-layouts: 1.41 us -> none  [on_device(): grads[1].transpose(0, 2, 1)]
    convert_element_type x1 -> x0, other arithmetic: 1.36 us -> none  [on_device(): grads = grads[:, :27].astype(F32)]
where the time goes in v3:
time: 84.8 us; the launch traced here: 84.6 us
  Pallas kernels  79.6 us (94%)
  local copies, waits for them, and re-layouts  4.35 us (5%)
    pallas_call x1, Pallas kernels, on_device(): pl.pallas_call(kernel, out_shape=(jax.ShapeDtypeStruct((64, 2, 16, 128),...  79.6 us
    unnamed x7, local copies, waits for them, and re-layouts  4.35 us

profile of v3, /device:TPU:1, one launch (start us, length us, event | category | flops | bytes accessed | tf_op | source)
XLA Modules:
  0.0 84.6 jit_solution(14921196396461629568)
XLA Ops:
  0.6 79.6 %conv_step.1 = (bf16[64,2,16,128]{3,2,1,0:T(8,128)(2,1)}, f32[27,64,128]{2,1,0:T(8,128)}, f32[27,64,128]{2,1,0:T(8,128)}) custom-call(bf16[64,4,8,256]{3,2,1,0:T(8,128)(2,1)} %bitcast.5, bf16[27,64,128]{2,1,0:T(8,128)(2,1)} %bitcast.9, bf16[27,64,128]{2,1,0:T(8,128)(2,1)} %wd_own.1, bf16[64,2,16,128]{3,2,1,0:T(8,128)(2,1)} %bitcast.7), custom_call_target="tpu_custom_call" | custom-call | tf_op jit(solution)/shard_map/conv_step/pallas_call | solution.py:589
  80.2 0.0 copy-start.1
  80.2 1.9 %copy.10 = bf16[1,64,2,16,128]{4,3,2,1,0:T(8,128)(2,1)} copy(bf16[1,64,2,16,128]{4,3,2,1,0:T(8,128)(2,1)} %bitcast.8) | data formatting | bytes 1048576
  82.2 0.0 copy-done.1
  82.2 0.0 copy-start
  82.2 0.9 %copy.11 = f32[27,64,128]{2,1,0:T(8,128)} copy(f32[27,64,128]{2,1,0:T(8,128)S(1)} %copy-done.1) | data formatting | bytes 1769472
  83.1 0.6 copy-done
  83.7 0.9 %copy.12 = f32[27,128,64]{1,2,0:T(8,128)} copy(f32[27,128,64]{1,2,0:T(8,128)S(1)} %bitcast.6) | data formatting | bytes 1769472
Async XLA Ops:
  80.2 2.0 %copy-start.1 = (f32[27,64,128]{2,1,0:T(8,128)S(1)}, f32[27,64,128]{2,1,0:T(8,128)}, u32[]{:S(2)}) copy-start(f32[27,64,128]{2,1,0:T(8,128)} %get-tuple-element.13) | copy-start | bytes 2654212
  82.2 1.5 %copy-start = (f32[27,64,128]{2,1,0:T(8,128)S(1)}, f32[27,64,128]{2,1,0:T(8,128)}, u32[]{:S(2)}) copy-start(f32[27,64,128]{2,1,0:T(8,128)} %get-tuple-element.8) | copy-start | bytes 2654212

commit v4 on v3

--- a/solution.py
+++ b/solution.py
@@ -106,31 +106,26 @@
     total = None
     for a in shifts:
         for e in range(3):
-            lanes = pl.ds(pl.multiple_of((2 * Y + e) * 128, 128), 256)
-            term = dot(w9[3 * a + e], taps_in[x + a, :, lanes])
+            term = dot(w9[3 * a + e], taps_in[x + a, :, (2 * Y + e) * 128 : (2 * Y + e + 2) * 128])
             total = term if total is None else total + term
     return total
 
 
 def early_activation(pre, slopes, x, Y):
     s = sigmoid(pre)
-    slopes[x, :, pl.ds(pl.multiple_of(Y * 256, 256), 256)] = s * (1.0 + pre * (1.0 - s))
+    slopes[x, :, Y * 256 : (Y + 1) * 256] = s * (1.0 + pre * (1.0 - s))
     act = pre * s
     act = act[:128] + act[128:]
     return act[:, :128] + act[:, 128:]
 
 
-def early_inner(taps_in, w9, slopes, pool_sum, first, last):
-    def body(Y, carry):
-        own = pl.ds(pl.multiple_of(Y * 256, 256), 256)
+def early_inner(taps_in, w9, slopes, pool_sum, Ys):
+    for Y in Ys:
         for x, shifts in ((0, (1, 2)), (3, (0, 1))):
-            slopes[x, :, own] = early_terms(taps_in, w9, x, Y, shifts)
+            slopes[x, :, Y * 256 : (Y + 1) * 256] = early_terms(taps_in, w9, x, Y, shifts)
         for X, x in enumerate((1, 2)):
             pre = early_terms(taps_in, w9, x, Y, (0, 1, 2))
-            pool_sum[X, :, pl.ds(pl.multiple_of(Y * 128, 128), 128)] = early_activation(pre, slopes, x, Y)
-        return carry
-
-    lax.fori_loop(first, last, body, 0)
+            pool_sum[X, :, Y * 128 : (Y + 1) * 128] = early_activation(pre, slopes, x, Y)
 
 
 def early_outer(taps_in, w9, slopes, pool_sum, pooled):
@@ -241,41 +236,37 @@
                         early_in[x, rows, lanes] = (here * slopes[x, rows, lanes]).astype(BF16)
 
 
+def slot(ae, f):
+    return 3 * ae + f + ae // 5
+
+
 def deep_gradient(deep_in, pooled, out):
-    def body(i, carry):
-        a, e = i // 3, i % 3
-        lanes = pl.ds(pl.multiple_of(e * 128, 128), 512)
+    for ae in range(9):
+        a, e = ae // 3, ae % 3
         total = None
         for X in range(2):
-            term = dot_nt(deep_in[X, :, 256:768], pooled[X + a, :, lanes])
+            term = dot_nt(deep_in[X, :, 256:768], pooled[X + a, :, e * 128 : e * 128 + 512])
             total = term if total is None else total + term
         for f in range(3):
             tap = total[:, f * 128 : (f + 1) * 128].astype(BF16).reshape(4, 2, 32, 128)
             for h in range(2):
-                out[h, 3 * i + f] = tap[:, h]
-        return carry
-
-    lax.fori_loop(0, 9, body, 0)
-
-
-def early_gradient(early_in, taps_in, out):
-    def body(i, carry):
-        a, e = i // 3, i % 3
-        lanes = pl.ds(pl.multiple_of(e * 128, 128), 1024)
+                out[h, slot(ae, f)] = tap[:, h]
+
+
+def early_gradient(early_in, taps_in, out, first, last):
+    for ae in range(first, last):
+        a, e = ae // 3, ae % 3
         total = None
         for x in range(4):
-            term = dot_nt(taps_in[x + a, :, lanes], early_in[x])
+            term = dot_nt(taps_in[x + a, :, e * 128 : e * 128 + 1024], early_in[x])
             total = term if total is None else total + term
         total = (total[:192, :128] + total[64:, 128:]).astype(BF16)
         for f in range(3):
             for h in range(2):
-                out[h, 3 * i + f] = total[f * 64 + h * 32 : f * 64 + h * 32 + 32]
-        return carry
-
-    lax.fori_loop(0, 9, body, 0)
-
-
-def add_taps(count, out, terms):
+                out[h, slot(ae, f)] = total[f * 64 + h * 32 : f * 64 + h * 32 + 32]
+
+
+def add_taps(first, last, out, terms):
     def body(t, carry):
         total = None
         for term in terms:
@@ -284,16 +275,24 @@
         out(t, total.astype(BF16))
         return carry
 
-    lax.fori_loop(0, count, body, 0)
+    lax.fori_loop(first, last, body, 0)
+
+
+def total_of(own, others):
+    total = own.astype(F32)
+    for other in others:
+        total += other.astype(F32)
+    return total
 
 
 def kernel(
-    samples_raw, ef, wd_own, ct_raw,
-    act_out, dg_out, eg_out,
-    samples, ct_own, act_in, full, sample_ext, taps_in, w9, spread, slopes, pool_sum, pooled, wd, wdt, ct, pre_deep, act, deep_in,
+    samples_raw, ef_hbm, wd_hbm, ct_hbm,
+    act_in, full,
+    samples, ef, ct_raw, ct_own, sample_ext, taps_in, w9, spread, slopes, pool_sum, pooled, wd, wdt, ct, pre_deep, act, deep_in,
     pooled_grad, send_x, send_y, got_x, got_y, got_xy, early_in,
-    dg, dg_pair, dg_sum, dg_chan, eg, eg_pair, part, part_in, eg_chan,
-    halo_send, halo_recv, x_send, x_recv, chan_send, chan_recv, pair_send, pair_recv, plane_send, plane_recv,
+    dg, dg_pair, dg_b, dg_b_in, dg_b_sum, dg_b_chan, dg_a, dg_a_in, dg_a_sum, dg_a_plane,
+    eg, eg_pair, eg_sum, eg_plane, eg_chan,
+    halo_send, halo_recv, x_send, x_recv, chan_send, chan_recv, pair_send, pair_recv, plane_send, plane_recv, both_send, both_recv, load_sem,
 ):
     dp, space, chan = lax.axis_index("dp"), lax.axis_index("space"), lax.axis_index("chan")
     core, column = space % 2, space // 2
@@ -320,9 +319,24 @@
     for peer in peers:
         pl.semaphore_signal(barrier, inc=1, device_id=peer, device_id_type=MESH)
 
+    mine = pl.ds(pl.multiple_of(chan * 64, 64), 64)
+    half = pl.ds(pl.multiple_of(core * 32, 32), 32)
+    loads = [
+        pltpu.make_async_copy(src, dst, load_sem.at[n])
+        for n, (src, dst) in enumerate(((ef_hbm, ef), (ct_hbm, ct_raw), (wd_hbm, wd.at[pl.ds(0, 27), mine, :])))
+    ]
+    for load in loads:
+        load.start()
     cells_first(samples_raw, samples)
+    loads[0].wait()
     build_early_weights(ef, w9)
     spread[...] = selector(256, 512, lambda r, c: r == 2 * (c % 128) + c // 128 - 1)
+    loads[1].wait()
+    deep_cells_first(ct_raw, ct_own)
+    ct[:, :, mine, :] = ct_own[pl.ds(pl.multiple_of(chan * 4, 4), 4)]
+    loads[2].wait()
+    wd[27, mine, :] = jnp.zeros((64, 128), BF16)
+
     pl.semaphore_wait(barrier, len(peers))
 
     sends = []
@@ -391,40 +405,38 @@
                 ref[x, rows, :] = jnp.zeros((rows.stop - rows.start, width), BF16)
 
     sample_y, sample_x = halo(0, sample_view)
-    mine = pl.ds(pl.multiple_of(chan * 64, 64), 64)
-    half = pl.ds(pl.multiple_of(core * 32, 32), 32)
-    wd[0:27, mine, :] = wd_own[...]
-    wd[27, mine, :] = jnp.zeros((64, 128), BF16)
+
+    def some_of(c, taps, of_core):
+        return wd.at[taps, pl.ds(pl.multiple_of(c * 64 + of_core * 32, 32), 32), :]
+
+    my_taps = pl.ds(space // 4 * 7, 7)
+    wd_copies = over_chan(0, lambda c: some_of(chan, my_taps, core), lambda j: some_of(chan, my_taps, core))
     for x in range(4):
         place_taps(samples[x].reshape(512, 256), spread, taps_in, x + 1, 1, 8)
-    deep_cells_first(ct_raw, ct_own)
-    ct[:, :, mine, :] = ct_own[pl.ds(pl.multiple_of(chan * 4, 4), 4)]
-    part[:, 27:, :, :] = jnp.zeros((2, 5, 32, 128), BF16)
+    for h in range(2):
+        dg[h, 15] = jnp.zeros((4, 32, 128), BF16)
+        eg[h, 15] = jnp.zeros((32, 128), BF16)
+    dg_a_sum[12:16] = jnp.zeros((4, 32, 128), BF16)
+    eg_sum[28:32] = jnp.zeros((4, 32, 128), BF16)
     for X in range(2):
         for lanes in (slice(0, 256), slice(768, 1024)):
             deep_in[X, :, lanes] = jnp.zeros((256, 256), BF16)
 
+    early_inner(taps_in, w9, slopes, pool_sum, (1, 2))
     landed(sample_y)
-
-    def some_of(c, taps, of_core):
-        return wd.at[taps, pl.ds(pl.multiple_of(c * 64 + of_core * 32, 32), 32), :]
-
-    my_taps = pl.ds(space // 4 * 7, 7)
-    wd_copies = over_chan(0, lambda c: some_of(chan, my_taps, core), lambda j: some_of(chan, my_taps, core))
-    ct_copies = over_chan(
-        1, lambda c: ct_own.at[pl.ds(pl.multiple_of(c * 4, 4), 4)], lambda j: ct.at[:, :, mine, :]
-    )
     for y in (0, 9):
         for x in range(1, 5):
             place_taps(sample_ext[x, y], spread, taps_in, x, y, 1)
     clear_y(taps_in, range(1, 5), slice(0, 256), 128)
-    early_inner(taps_in, w9, slopes, pool_sum, 0, 1)
     for j, copy in zip((1, 2, 3), wd_copies):
         landed([copy])
         block = some_of((chan - j + 4) % 4, my_taps, core)
         for i in (1, 2, 3):
             remote(block, block, x_send.at[j, i], x_recv.at[j, i], x_device(i))
-    early_inner(taps_in, w9, slopes, pool_sum, 1, 4)
+    ct_copies = over_chan(
+        1, lambda c: ct_own.at[pl.ds(pl.multiple_of(c * 4, 4), 4)], lambda j: ct.at[:, :, mine, :]
+    )
+    early_inner(taps_in, w9, slopes, pool_sum, (0, 3))
     landed(sample_x)
     for x in (0, 5):
         place_taps(sample_ext[x].reshape(640, 256), spread, taps_in, x, 0, 10)
@@ -474,16 +486,21 @@
             remote(send_y.at[n], got_y.at[1 - n], halo_send.at[2, k], halo_recv.at[2, k], side_device(0, dy))
         )
 
+    here = pl.ds(pl.multiple_of(chan * 4, 4), 4)
+    act_copies = over_chan(
+        4, lambda c: act.at[:, :, pl.ds(pl.multiple_of(c * 64, 64), 64), :], lambda j: act_in.at[here]
+    )
+    act_in[here] = act[:, :, mine, :]
+
+    def over_plane(n, src, dst):
+        return [
+            remote(src((rank + j) % 16), dst(j), plane_send.at[n, j], plane_recv.at[n, j], plane_device(j))
+            for j in range(1, 16)
+        ]
+
     deep_gradient(deep_in, pooled, dg)
-    dg_pair_copy = pair(0, dg.at[1 - core], dg_pair)
+    dg_pair_copy = pair(0, dg.at[1 - core, pl.ds(0, 28)], dg_pair)
     pooled_inner(deep_in, wdt, pooled_grad, (2,))
-
-    def put_sum(t, value):
-        dg_sum[:, t] = value
-
-    landed([dg_pair_copy])
-    add_taps(27, put_sum, [lambda t: dg[core, t], lambda t: dg_pair[t]])
-    dg_copies = over_chan(3, lambda c: dg_sum.at[c], lambda j: dg_chan.at[j])
     landed(grad_copies)
     for at, n in ((0, 0), (15, 1)):
 
@@ -501,105 +518,121 @@
                 got_xy[m, n] = jnp.zeros((128, 128), BF16)
 
     early_cotangent(pooled_grad, got_x, got_y, got_xy, slopes, early_in)
-    early_gradient(early_in, taps_in, eg)
-    eg_pair_copy = pair(1, eg.at[1 - core], eg_pair)
-
-    def put_part(n):
-        def put(t, value):
-            part[n, t] = value
-
-        return put
-
-    def taps_of(r):
-        return pl.ds(r * 2, 2)
-
-    own = taps_of(rank)
-
-    def plane_scatter(n):
-        copies = []
+    landed([dg_pair_copy])
+
+    def put_b(t, value):
+        dg_b[t] = value
+
+    def put_a(t, value):
+        dg_a[:, t - 16] = value
+
+    add_taps(16, 28, put_a, [lambda t: dg[core, t], lambda t: dg_pair[t]])
+    dg_a_copies = over_chan(3, lambda c: dg_a.at[c], lambda j: dg_a_in.at[j])
+    add_taps(0, 16, put_b, [lambda t: dg[core, t], lambda t: dg_pair[t]])
+    dg_b_copies = over_plane(0, lambda r: dg_b.at[r], lambda j: dg_b_in.at[j])
+    early_gradient(early_in, taps_in, eg, 0, 5)
+    eg_pair_0 = pair(1, eg.at[1 - core, pl.ds(0, 16)], eg_pair.at[pl.ds(0, 16)])
+    early_gradient(early_in, taps_in, eg, 5, 7)
+
+    def put_eg(t, value):
+        eg_sum[t] = value
+
+    landed([eg_pair_0])
+    add_taps(0, 16, put_eg, [lambda t: eg[core, t], lambda t: eg_pair[t]])
+    eg_copies = over_plane(2, lambda r: eg_sum.at[r], lambda j: eg_plane.at[0, j])
+    early_gradient(early_in, taps_in, eg, 7, 9)
+    eg_pair_1 = pair(2, eg.at[1 - core, pl.ds(16, 12)], eg_pair.at[pl.ds(16, 12)])
+
+    def put_a_sum(t, value):
+        dg_a_sum[t] = value
+
+    landed(dg_a_copies)
+    add_taps(0, 12, put_a_sum, [lambda t: dg_a[chan, t]] + [lambda t, j=j: dg_a_in[j, t] for j in (1, 2, 3)])
+    landed([eg_pair_1])
+    add_taps(16, 28, put_eg, [lambda t: eg[core, t], lambda t: eg_pair[t]])
+    eg_copies += over_plane(3, lambda r: eg_sum.at[16 + r], lambda j: eg_plane.at[1, j])
+    dg_a_copies = over_plane(1, lambda r: dg_a_sum.at[r], lambda j: dg_a_plane.at[j])
+    landed(dg_b_copies)
+    dg_b_sum[...] = total_of(dg_b[rank], [dg_b_in[j] for j in range(1, 16)])
+    dg_b_copies = over_chan(6, lambda c: dg_b_sum.at[c], lambda j: dg_b_chan.at[j])
+
+    def both(n, j, block):
+        remote(block, block, both_send.at[n, j], both_recv.at[n, j], sibling)
+
+    def gather(n):
+        block = full.at[n, :, rank, half, :]
         for j in range(1, 16):
-            src = part.at[n, taps_of((rank + j) % 16)]
-            copies.append(remote(src, part_in.at[n, j], plane_send.at[n, j], plane_recv.at[n, j], plane_device(j)))
-        return copies
-
-    def plane_sum(n):
-        summed = part[n, own].astype(F32)
+            remote(block, block, plane_send.at[4 + n, j], plane_recv.at[4 + n, j], plane_device(j))
+        both(n, 0, block)
+
+    def gathered(n):
         for j in range(1, 16):
-            summed += part_in[n, j].astype(F32)
-        return summed
-
-    def plane_gather(n):
-        block = full.at[n, own, half, :]
-        for j in range(1, 16):
-            remote(block, block, plane_send.at[2 + n, j], plane_recv.at[2 + n, j], plane_device(j))
-
-    def plane_gathered(n):
-        for j in range(1, 16):
-            theirs = full.at[n, taps_of((rank - j + 16) % 16), half, :]
-            describe(theirs, theirs, plane_send.at[2 + n, j], plane_recv.at[2 + n, j], plane_device(j)).wait_recv()
-
-    def halves(n):
-        block = full.at[n, pl.ds(0, 27), half, :]
-        pair(2 + n, block, block)
+            theirs = full.at[n, :, (rank - j + 16) % 16, half, :]
+            describe(theirs, theirs, plane_send.at[4 + n, j], plane_recv.at[4 + n, j], plane_device(j)).wait_recv()
+            both(n, j, theirs)
 
     def halves_landed(n):
-        block = full.at[n, pl.ds(0, 27), pl.ds(pl.multiple_of(32 - core * 32, 32), 32), :]
-        describe(block, block, pair_send.at[2 + n], pair_recv.at[2 + n], sibling).wait_recv()
-
-    landed([eg_pair_copy])
-    add_taps(27, put_part(1), [lambda t: eg[core, t], lambda t: eg_pair[t]])
-    eg_copies = plane_scatter(1)
-    landed(dg_copies)
-    add_taps(27, put_part(0), [lambda t: dg_sum[chan, t]] + [lambda t, j=j: dg_chan[j, t] for j in (1, 2, 3)])
-    dg_plane = plane_scatter(0)
-    here = pl.ds(pl.multiple_of(chan * 4, 4), 4)
-    act_copies = over_chan(
-        4, lambda c: act.at[:, :, pl.ds(pl.multiple_of(c * 64, 64), 64), :], lambda j: act_in.at[here]
-    )
-    act_in[here] = act[:, :, mine, :]
+        other = pl.ds(pl.multiple_of(32 - core * 32, 32), 32)
+        for j in range(16):
+            theirs = full.at[n, :, (rank - j + 16) % 16, other, :]
+            describe(theirs, theirs, both_send.at[n, j], both_recv.at[n, j], sibling).wait_recv()
+
     landed(eg_copies)
-    eg_chan[chan] = plane_sum(1)
+    for n in range(2):
+        eg_chan[chan, n] = total_of(eg_sum[16 * n + rank], [eg_plane[n, j] for j in range(1, 16)])
     over_chan(5, lambda c: eg_chan.at[chan], lambda j: eg_chan.at[chan])
-    landed(dg_plane)
-    full[0, own, half, :] = plane_sum(0).astype(BF16)
-    plane_gather(0)
+    landed(dg_a_copies)
+    landed(dg_b_copies)
+    full[0, 0, rank, half, :] = total_of(dg_b_sum[chan], [dg_b_chan[j] for j in (1, 2, 3)]).astype(BF16)
+    full[0, 1, rank, half, :] = total_of(dg_a_sum[rank], [dg_a_plane[j] for j in range(1, 16)]).astype(BF16)
     for j in (1, 2, 3):
         block = eg_chan.at[(chan - j + 4) % 4]
         describe(block, block, chan_send.at[5, j], chan_recv.at[5, j], chan_device(j)).wait_recv()
-    full[1, own, half, :] = ((eg_chan[0] + eg_chan[1]) + (eg_chan[2] + eg_chan[3])).astype(BF16)
-    plane_gather(1)
-    plane_gathered(0)
-    halves(0)
+    for n in range(2):
+        total = (eg_chan[0, n] + eg_chan[1, n]) + (eg_chan[2, n] + eg_chan[3, n])
+        full[1, n, rank, half, :] = total.astype(BF16)
+    gather(1)
+    gather(0)
+    gathered(1)
+    gathered(0)
+    halves_landed(1)
+    halves_landed(0)
+
     landed(act_copies)
-    deep_channels_first(act_in, act_out)
-    plane_gathered(1)
-    halves(1)
-    halves_landed(0)
-    for t in range(27):
-        dg_out[t] = full[0, t].astype(F32)
-    halves_landed(1)
-    for t in range(27):
-        eg_out[t] = full[1, t].astype(F32)
-
     for copy in sends:
         copy.wait_send()
 
 
+def finish(act_hbm, grads_hbm, act_out, dg_out, eg_out, act_in, grads, sem):
+    copies = [
+        pltpu.make_async_copy(grads_hbm.at[0], grads.at[0], sem.at[0]),
+        pltpu.make_async_copy(grads_hbm.at[1], grads.at[1], sem.at[1]),
+        pltpu.make_async_copy(act_hbm, act_in, sem.at[2]),
+    ]
+    for copy in copies:
+        copy.start()
+    for n, out in enumerate((dg_out, eg_out)):
+        copies[n].wait()
+        for t in range(27):
+            out[t] = grads[n, t // 15, t % 15].astype(F32)
+    copies[2].wait()
+    deep_channels_first(act_in, act_out)
+
+
 def on_device(samples, early_filters, deep_filters, deep_cotangent):
-    act, deep_grad, early_grad = pl.pallas_call(
+    act, grads = pl.pallas_call(
         kernel,
         out_shape=(
-            jax.ShapeDtypeStruct((64, 2, 16, 128), BF16),
-            jax.ShapeDtypeStruct((27, 64, 128), F32),
-            jax.ShapeDtypeStruct((27, 64, 128), F32),
+            jax.ShapeDtypeStruct((16, 2, 64, 128), BF16),
+            jax.ShapeDtypeStruct((2, 2, 16, 64, 128), BF16),
         ),
-        in_specs=[pl.BlockSpec(memory_space=pltpu.VMEM)] * 4,
-        out_specs=[pl.BlockSpec(memory_space=pltpu.VMEM)] * 3,
+        in_specs=[pl.BlockSpec(memory_space=pltpu.VMEM)] + [pl.BlockSpec(memory_space=pl.ANY)] * 3,
+        out_specs=[pl.BlockSpec(memory_space=pltpu.VMEM)] * 2,
         scratch_shapes=[
             pltpu.VMEM((4, 8, 64, 256), BF16),
+            pltpu.VMEM((27, 64, 128), BF16),
+            pltpu.VMEM((64, 2, 16, 128), BF16),
             pltpu.VMEM((16, 2, 64, 128), BF16),
-            pltpu.VMEM((16, 2, 64, 128), BF16),
-            pltpu.VMEM((2, 32, 64, 128), BF16),
             pltpu.VMEM((6, 10, 64, 256), BF16),
             pltpu.VMEM((6, 256, 1280), BF16),
             pltpu.VMEM((9, 256, 256), BF16),
@@ -620,31 +653,57 @@
             pltpu.VMEM((2, 2, 128, 128), BF16),
             pltpu.VMEM((2, 2, 128, 128), BF16),
             pltpu.VMEM((4, 256, 1024), BF16),
-            pltpu.VMEM((2, 27, 4, 32, 128), BF16),
-            pltpu.VMEM((27, 4, 32, 128), BF16),
-            pltpu.VMEM((4, 27, 32, 128), BF16),
-            pltpu.VMEM((4, 27, 32, 128), BF16),
-            pltpu.VMEM((2, 27, 32, 128), BF16),
-            pltpu.VMEM((27, 32, 128), BF16),
-            pltpu.VMEM((2, 32, 32, 128), BF16),
-            pltpu.VMEM((2, 16, 2, 32, 128), BF16),
+            pltpu.VMEM((2, 28, 4, 32, 128), BF16),
+            pltpu.VMEM((28, 4, 32, 128), BF16),
+            pltpu.VMEM((16, 4, 32, 128), BF16),
+            pltpu.VMEM((16, 4, 32, 128), BF16),
+            pltpu.VMEM((4, 32, 128), F32),
+            pltpu.VMEM((4, 32, 128), F32),
+            pltpu.VMEM((4, 12, 32, 128), BF16),
+            pltpu.VMEM((4, 12, 32, 128), BF16),
+            pltpu.VMEM((16, 32, 128), BF16),
+            pltpu.VMEM((16, 32, 128), BF16),
+            pltpu.VMEM((2, 28, 32, 128), BF16),
+            pltpu.VMEM((28, 32, 128), BF16),
+            pltpu.VMEM((32, 32, 128), BF16),
+            pltpu.VMEM((2, 16, 32, 128), BF16),
             pltpu.VMEM((4, 2, 32, 128), F32),
             pltpu.SemaphoreType.DMA((3, 8)),
             pltpu.SemaphoreType.DMA((3, 8)),
             pltpu.SemaphoreType.DMA((4, 4)),
             pltpu.SemaphoreType.DMA((4, 4)),
-            pltpu.SemaphoreType.DMA((6, 4)),
-            pltpu.SemaphoreType.DMA((6, 4)),
-            pltpu.SemaphoreType.DMA((4,)),
-            pltpu.SemaphoreType.DMA((4,)),
-            pltpu.SemaphoreType.DMA((4, 16)),
-            pltpu.SemaphoreType.DMA((4, 16)),
+            pltpu.SemaphoreType.DMA((7, 4)),
+            pltpu.SemaphoreType.DMA((7, 4)),
+            pltpu.SemaphoreType.DMA((3,)),
+            pltpu.SemaphoreType.DMA((3,)),
+            pltpu.SemaphoreType.DMA((6, 16)),
+            pltpu.SemaphoreType.DMA((6, 16)),
+            pltpu.SemaphoreType.DMA((2, 16)),
+            pltpu.SemaphoreType.DMA((2, 16)),
+            pltpu.SemaphoreType.DMA((3,)),
         ],
         compiler_params=pltpu.CompilerParams(
             collective_id=0, has_side_effects=True, vmem_limit_bytes=56 * 1024 * 1024
         ),
         name="conv_step",
     )(samples[0], early_filters.transpose(0, 2, 1), deep_filters, deep_cotangent[0])
+    act, deep_grad, early_grad = pl.pallas_call(
+        finish,
+        out_shape=(
+            jax.ShapeDtypeStruct((64, 2, 16, 128), BF16),
+            jax.ShapeDtypeStruct((27, 64, 128), F32),
+            jax.ShapeDtypeStruct((27, 64, 128), F32),
+        ),
+        in_specs=[pl.BlockSpec(memory_space=pl.ANY)] * 2,
+        out_specs=[pl.BlockSpec(memory_space=pltpu.VMEM)] * 3,
+        scratch_shapes=[
+            pltpu.VMEM((16, 2, 64, 128), BF16),
+            pltpu.VMEM((2, 2, 16, 64, 128), BF16),
+            pltpu.SemaphoreType.DMA((3,)),
+        ],
+        compiler_params=pltpu.CompilerParams(vmem_limit_bytes=56 * 1024 * 1024),
+        name="finish",
+    )(act, grads)
     return act[None], deep_grad, early_grad.transpose(0, 2, 1)
 
 

time: 84.8 us -> 80.5 us (0.949)
  local copies, waits for them, and re-layouts: 4.35 us -> 0 us
    unnamed x7 -> x0, local copies, waits for them, and re-layouts: 4.35 us -> none
    pallas_call x1 -> x2, Pallas kernels: 79.6 us -> 79.5 us  [the longest x1 76.8 us: on_device(): pl.pallas_call(kernel, out_shape=(jax.ShapeDtypeStruct((16, 2, 64, 128),...]
where the time goes in v4:
time: 80.5 us; the launch traced here: 80.3 us
  Pallas kernels  79.5 us (99%)
  between operations  0.82 us (1%)
    pallas_call x1, Pallas kernels, on_device(): pl.pallas_call(kernel, out_shape=(jax.ShapeDtypeStruct((16, 2, 64, 128),...  76.8 us
    pallas_call x1, Pallas kernels, on_device(): pl.pallas_call(finish, out_shape=(jax.ShapeDtypeStruct((64, 2, 16, 128),...  2.76 us

profile of v4, /device:TPU:1, one launch (start us, length us, event | category | flops | bytes accessed | tf_op | source)
XLA Modules:
  0.0 80.3 jit_solution(6886238124298593267)
XLA Ops:
  0.6 76.8 %conv_step.1 = (bf16[16,2,64,128]{3,2,1,0:T(8,128)(2,1)}, bf16[2,2,16,64,128]{4,3,2,1,0:T(8,128)(2,1)}) custom-call(bf16[64,4,8,256]{3,2,1,0:T(8,128)(2,1)} %bitcast.5, bf16[27,64,128]{2,1,0:T(8,128)(2,1)} %bitcast.7, bf16[27,64,128]{2,1,0:T(8,128)(2,1)} %wd_hbm.1, bf16[64,2,16,128]{3,2,1,0:T(8,128)(2,1)} %bitcast.6), custom_call_target="tpu_custom_call" | custom-call | tf_op jit(solution)/shard_map/conv_step/pallas_call | solution.py:623
  77.4 2.8 %finish.1 = (bf16[64,2,16,128]{3,2,1,0:T(8,128)(2,1)}, f32[27,64,128]{2,1,0:T(8,128)}, f32[27,64,128]{2,1,0:T(8,128)}) custom-call(bf16[16,2,64,128]{3,2,1,0:T(8,128)(2,1)} %get-tuple-element.8.act_hbm, bf16[2,2,16,64,128]{4,3,2,1,0:T(8,128)(2,1)} %get-tuple-element.9.grads_hbm), custom_call_target="tpu_custom_call" | custom-call | tf_op jit(solution)/shard_map/finish/pallas_call | solution.py:690

commit v5 on v4

--- a/solution.py
+++ b/solution.py
@@ -128,12 +128,12 @@
             pool_sum[X, :, Y * 128 : (Y + 1) * 128] = early_activation(pre, slopes, x, Y)
 
 
-def early_outer(taps_in, w9, slopes, pool_sum, pooled):
+def early_outer(taps_in, w9, slopes, pool_sum, pooled, X):
+    x, a = ((0, 0), (3, 2))[X]
     for Y in range(4):
-        for X, x, a in ((0, 0, 0), (1, 3, 2)):
-            pre = slopes[x, :, Y * 256 : (Y + 1) * 256] + early_terms(taps_in, w9, x, Y, (a,))
-            total = pool_sum[X, :, Y * 128 : (Y + 1) * 128] + early_activation(pre, slopes, x, Y)
-            pooled[X + 1, 128:256, (Y + 1) * 128 : (Y + 2) * 128] = (total * 0.125).astype(BF16)
+        pre = slopes[x, :, Y * 256 : (Y + 1) * 256] + early_terms(taps_in, w9, x, Y, (a,))
+        total = pool_sum[X, :, Y * 128 : (Y + 1) * 128] + early_activation(pre, slopes, x, Y)
+        pooled[X + 1, 128:256, (Y + 1) * 128 : (Y + 2) * 128] = (total * 0.125).astype(BF16)
 
 
 def shift_pooled(pooled, xs, first, count):
@@ -208,10 +208,10 @@
     return jnp.concatenate(parts, axis=1)
 
 
-def pooled_outer(deep_in, wdt, send_x):
-    for n, pairs in enumerate((((0, 0),), ((1, 2),))):
-        for first in (0, 2, 4):
-            send_x[n, :, first * 128 : (first + 2) * 128] = pooled_terms(deep_in, wdt, pairs, first).astype(BF16)
+def pooled_outer(deep_in, wdt, send_x, n):
+    for first in (0, 2, 4):
+        terms = pooled_terms(deep_in, wdt, (((0, 0),), ((1, 2),))[n], first)
+        send_x[n, :, first * 128 : (first + 2) * 128] = terms.astype(BF16)
 
 
 def pooled_inner(deep_in, wdt, pooled_grad, firsts):
@@ -292,7 +292,7 @@
     pooled_grad, send_x, send_y, got_x, got_y, got_xy, early_in,
     dg, dg_pair, dg_b, dg_b_in, dg_b_sum, dg_b_chan, dg_a, dg_a_in, dg_a_sum, dg_a_plane,
     eg, eg_pair, eg_sum, eg_plane, eg_chan,
-    halo_send, halo_recv, x_send, x_recv, chan_send, chan_recv, pair_send, pair_recv, plane_send, plane_recv, both_send, both_recv, load_sem,
+    halo_send, halo_recv, x_send, x_recv, piece_send, piece_recv, chan_send, chan_recv, pair_send, pair_recv, plane_send, plane_recv, both_send, both_recv, load_sem,
 ):
     dp, space, chan = lax.axis_index("dp"), lax.axis_index("space"), lax.axis_index("chan")
     core, column = space % 2, space // 2
@@ -364,12 +364,15 @@
     def pair(n, src, dst):
         return remote(src, dst, pair_send.at[n], pair_recv.at[n], sibling)
 
-    def halo(n, view):
-        copies = {}
-        for k, (dx, dy) in enumerate(SIDES):
-            src, dst = view(dx, dy)
-            copies[dx, dy] = remote(src, dst, halo_send.at[n, k], halo_recv.at[n, k], side_device(dx, dy))
-        return [copies[0, -1], copies[0, 1]], [copy for (dx, _), copy in copies.items() if dx != 0]
+    def halo(n, view, dxs):
+        copies = []
+        for dx in dxs:
+            for dy in (-1, 0, 1):
+                if (dx, dy) != (0, 0):
+                    src, dst = view(dx, dy)
+                    k = SIDES.index((dx, dy))
+                    copies.append(remote(src, dst, halo_send.at[n, k], halo_recv.at[n, k], side_device(dx, dy)))
+        return copies
 
     def sample_view(dx, dy):
         (sx, nx), (tx, _) = sent_and_landed(dx, 4)
@@ -404,7 +407,8 @@
             def _():
                 ref[x, rows, :] = jnp.zeros((rows.stop - rows.start, width), BF16)
 
-    sample_y, sample_x = halo(0, sample_view)
+    sample_y = halo(0, sample_view, (0,))
+    sample_x = halo(0, sample_view, (-1, 1))
 
     def some_of(c, taps, of_core):
         return wd.at[taps, pl.ds(pl.multiple_of(c * 64 + of_core * 32, 32), 32), :]
@@ -433,6 +437,7 @@
         block = some_of((chan - j + 4) % 4, my_taps, core)
         for i in (1, 2, 3):
             remote(block, block, x_send.at[j, i], x_recv.at[j, i], x_device(i))
+        remote(block, block, piece_send.at[j, 0], piece_recv.at[j, 0], sibling)
     ct_copies = over_chan(
         1, lambda c: ct_own.at[pl.ds(pl.multiple_of(c * 4, 4), 4)], lambda j: ct.at[:, :, mine, :]
     )
@@ -442,23 +447,25 @@
         place_taps(sample_ext[x].reshape(640, 256), spread, taps_in, x, 0, 10)
     clear_y(taps_in, (0, 5), slice(0, 256), 128)
     clear_x(taps_in, slice(0, 256))
-    early_outer(taps_in, w9, slopes, pool_sum, pooled)
-
-    pooled_y, pooled_x = halo(1, field_view(pooled, 128, 128))
+    early_outer(taps_in, w9, slopes, pool_sum, pooled, 0)
+    pooled_x = halo(1, field_view(pooled, 128, 128), (-1,))
+    early_outer(taps_in, w9, slopes, pool_sum, pooled, 1)
+    pooled_x += halo(1, field_view(pooled, 128, 128), (1,))
+    pooled_y = halo(1, field_view(pooled, 128, 128), (0,))
     shift_pooled(pooled, (1, 2), 1, 4)
     for j in (1, 2, 3):
         for i in (1, 2, 3):
             block = some_of((chan - j + 4) % 4, pl.ds((space // 4 - i + 4) % 4 * 7, 7), core)
             describe(block, block, x_send.at[j, i], x_recv.at[j, i], x_device(i)).wait_recv()
-        block = some_of((chan - j + 4) % 4, pl.ds(0, 27), core)
-        remote(block, block, chan_send.at[2, j], chan_recv.at[2, j], sibling)
+            remote(block, block, piece_send.at[j, i], piece_recv.at[j, i], sibling)
     landed(pooled_y)
     clear_y(pooled, (1, 2), slice(128, 256), 128)
     shift_pooled(pooled, (1, 2), 0, 1)
     shift_pooled(pooled, (1, 2), 5, 1)
     for j in (1, 2, 3):
-        block = some_of((chan - j + 4) % 4, pl.ds(0, 27), 1 - core)
-        describe(block, block, chan_send.at[2, j], chan_recv.at[2, j], sibling).wait_recv()
+        for i in range(4):
+            block = some_of((chan - j + 4) % 4, pl.ds((space // 4 - i + 4) % 4 * 7, 7), 1 - core)
+            describe(block, block, piece_send.at[j, i], piece_recv.at[j, i], sibling).wait_recv()
     deep_inner(pooled, wd, pre_deep)
     transpose_deep_weights(wd, wdt)
     landed(pooled_x)
@@ -468,9 +475,9 @@
     landed(ct_copies)
     deep_outer(pooled, wd, ct, pre_deep, act, deep_in)
 
-    pooled_outer(deep_in, wdt, send_x)
     grad_copies = []
     for n, dx in enumerate((-1, 1)):
+        pooled_outer(deep_in, wdt, send_x, n)
         for dy in (-1, 0, 1):
             at, count = {-1: (0, 1), 0: (1, 4), 1: (5, 1)}[dy]
             src = send_x.at[n, :, pl.ds(at * 128, count * 128)]
@@ -539,7 +546,7 @@
 
     landed([eg_pair_0])
     add_taps(0, 16, put_eg, [lambda t: eg[core, t], lambda t: eg_pair[t]])
-    eg_copies = over_plane(2, lambda r: eg_sum.at[r], lambda j: eg_plane.at[0, j])
+    eg_copies = [over_plane(2, lambda r: eg_sum.at[r], lambda j: eg_plane.at[0, j])]
     early_gradient(early_in, taps_in, eg, 7, 9)
     eg_pair_1 = pair(2, eg.at[1 - core, pl.ds(16, 12)], eg_pair.at[pl.ds(16, 12)])
 
@@ -550,7 +557,7 @@
     add_taps(0, 12, put_a_sum, [lambda t: dg_a[chan, t]] + [lambda t, j=j: dg_a_in[j, t] for j in (1, 2, 3)])
     landed([eg_pair_1])
     add_taps(16, 28, put_eg, [lambda t: eg[core, t], lambda t: eg_pair[t]])
-    eg_copies += over_plane(3, lambda r: eg_sum.at[16 + r], lambda j: eg_plane.at[1, j])
+    eg_copies.append(over_plane(3, lambda r: eg_sum.at[16 + r], lambda j: eg_plane.at[1, j]))
     dg_a_copies = over_plane(1, lambda r: dg_a_sum.at[r], lambda j: dg_a_plane.at[j])
     landed(dg_b_copies)
     dg_b_sum[...] = total_of(dg_b[rank], [dg_b_in[j] for j in range(1, 16)])
@@ -577,26 +584,33 @@
             theirs = full.at[n, :, (rank - j + 16) % 16, other, :]
             describe(theirs, theirs, both_send.at[n, j], both_recv.at[n, j], sibling).wait_recv()
 
-    landed(eg_copies)
-    for n in range(2):
+    def chan_terms(n):
+        landed(eg_copies[n])
         eg_chan[chan, n] = total_of(eg_sum[16 * n + rank], [eg_plane[n, j] for j in range(1, 16)])
-    over_chan(5, lambda c: eg_chan.at[chan], lambda j: eg_chan.at[chan])
-    landed(dg_a_copies)
+        over_chan((5, 2)[n], lambda c: eg_chan.at[chan, n], lambda j: eg_chan.at[chan, n])
+
+    def chan_total(n):
+        for j in (1, 2, 3):
+            block = eg_chan.at[(chan - j + 4) % 4, n]
+            k = (5, 2)[n]
+            describe(block, block, chan_send.at[k, j], chan_recv.at[k, j], chan_device(j)).wait_recv()
+        total = (eg_chan[0, n] + eg_chan[1, n]) + (eg_chan[2, n] + eg_chan[3, n])
+        full[1, n, rank, half, :] = total.astype(BF16)
+
+    chan_terms(0)
     landed(dg_b_copies)
     full[0, 0, rank, half, :] = total_of(dg_b_sum[chan], [dg_b_chan[j] for j in (1, 2, 3)]).astype(BF16)
+    landed(dg_a_copies)
     full[0, 1, rank, half, :] = total_of(dg_a_sum[rank], [dg_a_plane[j] for j in range(1, 16)]).astype(BF16)
-    for j in (1, 2, 3):
-        block = eg_chan.at[(chan - j + 4) % 4]
-        describe(block, block, chan_send.at[5, j], chan_recv.at[5, j], chan_device(j)).wait_recv()
-    for n in range(2):
-        total = (eg_chan[0, n] + eg_chan[1, n]) + (eg_chan[2, n] + eg_chan[3, n])
-        full[1, n, rank, half, :] = total.astype(BF16)
+    gather(0)
+    chan_terms(1)
+    chan_total(0)
+    chan_total(1)
     gather(1)
-    gather(0)
+    gathered(0)
     gathered(1)
-    gathered(0)
+    halves_landed(0)
     halves_landed(1)
-    halves_landed(0)
 
     landed(act_copies)
     for copy in sends:
@@ -672,6 +686,8 @@
             pltpu.SemaphoreType.DMA((3, 8)),
             pltpu.SemaphoreType.DMA((4, 4)),
             pltpu.SemaphoreType.DMA((4, 4)),
+            pltpu.SemaphoreType.DMA((4, 4)),
+            pltpu.SemaphoreType.DMA((4, 4)),
             pltpu.SemaphoreType.DMA((7, 4)),
             pltpu.SemaphoreType.DMA((7, 4)),
             pltpu.SemaphoreType.DMA((3,)),

time: 80.5 us -> 79.2 us (0.984)
  Pallas kernels: 79.5 us -> 78.2 us
    pallas_call x1, Pallas kernels: 76.8 us -> 75.5 us  [on_device(): pl.pallas_call(kernel, out_shape=(jax.ShapeDtypeStruct((16, 2, 64, 128),...]
where the time goes in v5:
time: 79.2 us; the launch traced here: 79 us
  Pallas kernels  78.2 us (99%)
  between operations  0.82 us (1%)
    pallas_call x1, Pallas kernels, on_device(): pl.pallas_call(kernel, out_shape=(jax.ShapeDtypeStruct((16, 2, 64, 128),...  75.5 us
    pallas_call x1, Pallas kernels, on_device(): pl.pallas_call(finish, out_shape=(jax.ShapeDtypeStruct((64, 2, 16, 128),...  2.76 us

profile of v5, /device:TPU:1, one launch (start us, length us, event | category | flops | bytes accessed | tf_op | source)
XLA Modules:
  0.0 79.0 jit_solution(8295458948905168815)
XLA Ops:
  0.6 75.5 %conv_step.1 = (bf16[16,2,64,128]{3,2,1,0:T(8,128)(2,1)}, bf16[2,2,16,64,128]{4,3,2,1,0:T(8,128)(2,1)}) custom-call(bf16[64,4,8,256]{3,2,1,0:T(8,128)(2,1)} %bitcast.5, bf16[27,64,128]{2,1,0:T(8,128)(2,1)} %bitcast.7, bf16[27,64,128]{2,1,0:T(8,128)(2,1)} %wd_hbm.1, bf16[64,2,16,128]{3,2,1,0:T(8,128)(2,1)} %bitcast.6), custom_call_target="tpu_custom_call" | custom-call | tf_op jit(solution)/shard_map/conv_step/pallas_call | solution.py:637
  76.1 2.8 %finish.1 = (bf16[64,2,16,128]{3,2,1,0:T(8,128)(2,1)}, f32[27,64,128]{2,1,0:T(8,128)}, f32[27,64,128]{2,1,0:T(8,128)}) custom-call(bf16[16,2,64,128]{3,2,1,0:T(8,128)(2,1)} %get-tuple-element.8.act_hbm, bf16[2,2,16,64,128]{4,3,2,1,0:T(8,128)(2,1)} %get-tuple-element.9.grads_hbm), custom_call_target="tpu_custom_call" | custom-call | tf_op jit(solution)/shard_map/finish/pallas_call | solution.py:706

commit v6 on v5

--- a/solution.py
+++ b/solution.py
@@ -407,7 +407,6 @@
             def _():
                 ref[x, rows, :] = jnp.zeros((rows.stop - rows.start, width), BF16)
 
-    sample_y = halo(0, sample_view, (0,))
     sample_x = halo(0, sample_view, (-1, 1))
 
     def some_of(c, taps, of_core):
@@ -415,6 +414,7 @@
 
     my_taps = pl.ds(space // 4 * 7, 7)
     wd_copies = over_chan(0, lambda c: some_of(chan, my_taps, core), lambda j: some_of(chan, my_taps, core))
+    sample_y = halo(0, sample_view, (0,))
     for x in range(4):
         place_taps(samples[x].reshape(512, 256), spread, taps_in, x + 1, 1, 8)
     for h in range(2):
@@ -427,17 +427,17 @@
             deep_in[X, :, lanes] = jnp.zeros((256, 256), BF16)
 
     early_inner(taps_in, w9, slopes, pool_sum, (1, 2))
-    landed(sample_y)
-    for y in (0, 9):
-        for x in range(1, 5):
-            place_taps(sample_ext[x, y], spread, taps_in, x, y, 1)
-    clear_y(taps_in, range(1, 5), slice(0, 256), 128)
     for j, copy in zip((1, 2, 3), wd_copies):
         landed([copy])
         block = some_of((chan - j + 4) % 4, my_taps, core)
         for i in (1, 2, 3):
             remote(block, block, x_send.at[j, i], x_recv.at[j, i], x_device(i))
         remote(block, block, piece_send.at[j, 0], piece_recv.at[j, 0], sibling)
+    landed(sample_y)
+    for y in (0, 9):
+        for x in range(1, 5):
+            place_taps(sample_ext[x, y], spread, taps_in, x, y, 1)
+    clear_y(taps_in, range(1, 5), slice(0, 256), 128)
     ct_copies = over_chan(
         1, lambda c: ct_own.at[pl.ds(pl.multiple_of(c * 4, 4), 4)], lambda j: ct.at[:, :, mine, :]
     )

time: 79.2 us -> 79.3 us (level)
  no operation moved by 1% of the time
where the time goes in v6:
time: 79.3 us; the launch traced here: 79.1 us
  Pallas kernels  78.3 us (99%)
  between operations  0.82 us (1%)
    pallas_call x1, Pallas kernels, on_device(): pl.pallas_call(kernel, out_shape=(jax.ShapeDtypeStruct((16, 2, 64, 128),...  75.5 us
    pallas_call x1, Pallas kernels, on_device(): pl.pallas_call(finish, out_shape=(jax.ShapeDtypeStruct((64, 2, 16, 128),...  2.76 us

profile of v6, /device:TPU:1, one launch (start us, length us, event | category | flops | bytes accessed | tf_op | source)
XLA Modules:
  0.0 79.1 jit_solution(441324470181051114)
XLA Ops:
  0.6 75.5 %conv_step.1 = (bf16[16,2,64,128]{3,2,1,0:T(8,128)(2,1)}, bf16[2,2,16,64,128]{4,3,2,1,0:T(8,128)(2,1)}) custom-call(bf16[64,4,8,256]{3,2,1,0:T(8,128)(2,1)} %bitcast.5, bf16[27,64,128]{2,1,0:T(8,128)(2,1)} %bitcast.7, bf16[27,64,128]{2,1,0:T(8,128)(2,1)} %wd_hbm.1, bf16[64,2,16,128]{3,2,1,0:T(8,128)(2,1)} %bitcast.6), custom_call_target="tpu_custom_call" | custom-call | tf_op jit(solution)/shard_map/conv_step/pallas_call | solution.py:637
  76.2 2.8 %finish.1 = (bf16[64,2,16,128]{3,2,1,0:T(8,128)(2,1)}, f32[27,64,128]{2,1,0:T(8,128)}, f32[27,64,128]{2,1,0:T(8,128)}) custom-call(bf16[16,2,64,128]{3,2,1,0:T(8,128)(2,1)} %get-tuple-element.8.act_hbm, bf16[2,2,16,64,128]{4,3,2,1,0:T(8,128)(2,1)} %get-tuple-element.9.grads_hbm), custom_call_target="tpu_custom_call" | custom-call | tf_op jit(solution)/shard_map/finish/pallas_call | solution.py:706

commit v7 on v6

--- a/solution.py
+++ b/solution.py
@@ -493,50 +493,50 @@
             remote(send_y.at[n], got_y.at[1 - n], halo_send.at[2, k], halo_recv.at[2, k], side_device(0, dy))
         )
 
+    def over_plane(n, src, dst):
+        return [
+            remote(src((rank + j) % 16), dst(j), plane_send.at[n, j], plane_recv.at[n, j], plane_device(j))
+            for j in range(1, 16)
+        ]
+
+    deep_gradient(deep_in, pooled, dg)
+    dg_pair_copy = pair(0, dg.at[1 - core, pl.ds(0, 28)], dg_pair)
+    pooled_inner(deep_in, wdt, pooled_grad, (2,))
+    landed(grad_copies)
+    for at, n in ((0, 0), (15, 1)):
+
+        @pl.when(space == at)
+        def _():
+            got_x[n] = jnp.zeros((128, 512), BF16)
+            got_xy[n] = jnp.zeros((2, 128, 128), BF16)
+
+    for at, n in ((0, 0), (3, 1)):
+
+        @pl.when(chan == at)
+        def _():
+            got_y[n] = jnp.zeros((2, 128, 128), BF16)
+            for m in range(2):
+                got_xy[m, n] = jnp.zeros((128, 128), BF16)
+
+    early_cotangent(pooled_grad, got_x, got_y, got_xy, slopes, early_in)
+    landed([dg_pair_copy])
+
+    def put_b(t, value):
+        dg_b[t] = value
+
+    def put_a(t, value):
+        dg_a[:, t - 16] = value
+
+    add_taps(16, 28, put_a, [lambda t: dg[core, t], lambda t: dg_pair[t]])
+    dg_a_copies = over_chan(3, lambda c: dg_a.at[c], lambda j: dg_a_in.at[j])
+    add_taps(0, 16, put_b, [lambda t: dg[core, t], lambda t: dg_pair[t]])
+    dg_b_copies = over_plane(0, lambda r: dg_b.at[r], lambda j: dg_b_in.at[j])
     here = pl.ds(pl.multiple_of(chan * 4, 4), 4)
     act_copies = over_chan(
         4, lambda c: act.at[:, :, pl.ds(pl.multiple_of(c * 64, 64), 64), :], lambda j: act_in.at[here]
     )
     act_in[here] = act[:, :, mine, :]
 
-    def over_plane(n, src, dst):
-        return [
-            remote(src((rank + j) % 16), dst(j), plane_send.at[n, j], plane_recv.at[n, j], plane_device(j))
-            for j in range(1, 16)
-        ]
-
-    deep_gradient(deep_in, pooled, dg)
-    dg_pair_copy = pair(0, dg.at[1 - core, pl.ds(0, 28)], dg_pair)
-    pooled_inner(deep_in, wdt, pooled_grad, (2,))
-    landed(grad_copies)
-    for at, n in ((0, 0), (15, 1)):
-
-        @pl.when(space == at)
-        def _():
-            got_x[n] = jnp.zeros((128, 512), BF16)
-            got_xy[n] = jnp.zeros((2, 128, 128), BF16)
-
-    for at, n in ((0, 0), (3, 1)):
-
-        @pl.when(chan == at)
-        def _():
-            got_y[n] = jnp.zeros((2, 128, 128), BF16)
-            for m in range(2):
-                got_xy[m, n] = jnp.zeros((128, 128), BF16)
-
-    early_cotangent(pooled_grad, got_x, got_y, got_xy, slopes, early_in)
-    landed([dg_pair_copy])
-
-    def put_b(t, value):
-        dg_b[t] = value
-
-    def put_a(t, value):
-        dg_a[:, t - 16] = value
-
-    add_taps(16, 28, put_a, [lambda t: dg[core, t], lambda t: dg_pair[t]])
-    dg_a_copies = over_chan(3, lambda c: dg_a.at[c], lambda j: dg_a_in.at[j])
-    add_taps(0, 16, put_b, [lambda t: dg[core, t], lambda t: dg_pair[t]])
-    dg_b_copies = over_plane(0, lambda r: dg_b.at[r], lambda j: dg_b_in.at[j])
     early_gradient(early_in, taps_in, eg, 0, 5)
     eg_pair_0 = pair(1, eg.at[1 - core, pl.ds(0, 16)], eg_pair.at[pl.ds(0, 16)])
     early_gradient(early_in, taps_in, eg, 5, 7)
@@ -617,20 +617,29 @@
         copy.wait_send()
 
 
-def finish(act_hbm, grads_hbm, act_out, dg_out, eg_out, act_in, grads, sem):
-    copies = [
+def finish(act_hbm, grads_hbm, act_out, dg_out, eg_out, act_in, grads, act, wide, sem):
+    loads = [
         pltpu.make_async_copy(grads_hbm.at[0], grads.at[0], sem.at[0]),
         pltpu.make_async_copy(grads_hbm.at[1], grads.at[1], sem.at[1]),
         pltpu.make_async_copy(act_hbm, act_in, sem.at[2]),
     ]
-    for copy in copies:
-        copy.start()
-    for n, out in enumerate((dg_out, eg_out)):
-        copies[n].wait()
+    stores = [
+        pltpu.make_async_copy(wide.at[0], dg_out, sem.at[3]),
+        pltpu.make_async_copy(wide.at[1], eg_out, sem.at[4]),
+        pltpu.make_async_copy(act, act_out, sem.at[5]),
+    ]
+    for load in loads:
+        load.start()
+    for n in range(2):
+        loads[n].wait()
         for t in range(27):
-            out[t] = grads[n, t // 15, t % 15].astype(F32)
-    copies[2].wait()
-    deep_channels_first(act_in, act_out)
+            wide[n, t] = grads[n, t // 15, t % 15].astype(F32)
+        stores[n].start()
+    loads[2].wait()
+    deep_channels_first(act_in, act)
+    stores[2].start()
+    for store in stores:
+        store.wait()
 
 
 def on_device(samples, early_filters, deep_filters, deep_cotangent):
@@ -711,11 +720,13 @@
             jax.ShapeDtypeStruct((27, 64, 128), F32),
         ),
         in_specs=[pl.BlockSpec(memory_space=pl.ANY)] * 2,
-        out_specs=[pl.BlockSpec(memory_space=pltpu.VMEM)] * 3,
+        out_specs=[pl.BlockSpec(memory_space=pl.ANY)] * 3,
         scratch_shapes=[
             pltpu.VMEM((16, 2, 64, 128), BF16),
             pltpu.VMEM((2, 2, 16, 64, 128), BF16),
-            pltpu.SemaphoreType.DMA((3,)),
+            pltpu.VMEM((64, 2, 16, 128), BF16),
+            pltpu.VMEM((2, 27, 64, 128), F32),
+            pltpu.SemaphoreType.DMA((6,)),
         ],
         compiler_params=pltpu.CompilerParams(vmem_limit_bytes=56 * 1024 * 1024),
         name="finish",

time: 79.3 us -> 77.7 us (0.980)
  Pallas kernels: 78.3 us -> 76.7 us
    pallas_call x1, Pallas kernels: 75.5 us -> 74.2 us  [on_device(): pl.pallas_call(kernel, out_shape=(jax.ShapeDtypeStruct((16, 2, 64, 128),...]
where the time goes in v7:
time: 77.7 us; the launch traced here: 77.6 us
  Pallas kernels  76.7 us (99%)
  between operations  0.82 us (1%)
    pallas_call x1, Pallas kernels, on_device(): pl.pallas_call(kernel, out_shape=(jax.ShapeDtypeStruct((16, 2, 64, 128),...  74.2 us
    pallas_call x1, Pallas kernels, on_device(): pl.pallas_call(finish, out_shape=(jax.ShapeDtypeStruct((64, 2, 16, 128),...  2.53 us

profile of v7, /device:TPU:1, one launch (start us, length us, event | category | flops | bytes accessed | tf_op | source)
XLA Modules:
  0.0 77.6 jit_solution(13696885324338941557)
XLA Ops:
  0.6 74.2 %conv_step.1 = (bf16[16,2,64,128]{3,2,1,0:T(8,128)(2,1)}, bf16[2,2,16,64,128]{4,3,2,1,0:T(8,128)(2,1)}) custom-call(bf16[64,4,8,256]{3,2,1,0:T(8,128)(2,1)} %bitcast.5, bf16[27,64,128]{2,1,0:T(8,128)(2,1)} %bitcast.7, bf16[27,64,128]{2,1,0:T(8,128)(2,1)} %wd_hbm.1, bf16[64,2,16,128]{3,2,1,0:T(8,128)(2,1)} %bitcast.6), custom_call_target="tpu_custom_call" | custom-call | tf_op jit(solution)/shard_map/conv_step/pallas_call | solution.py:646
  74.8 2.5 %finish.1 = (bf16[64,2,16,128]{3,2,1,0:T(8,128)(2,1)}, f32[27,64,128]{2,1,0:T(8,128)}, f32[27,64,128]{2,1,0:T(8,128)}) custom-call(bf16[16,2,64,128]{3,2,1,0:T(8,128)(2,1)} %get-tuple-element.8.act_hbm, bf16[2,2,16,64,128]{4,3,2,1,0:T(8,128)(2,1)} %get-tuple-element.9.grads_hbm), custom_call_target="tpu_custom_call" | custom-call | tf_op jit(solution)/shard_map/finish/pallas_call | solution.py:715
